TPU v7x, 128 devices: a whole 4x4x4 slice. The times are simulated.
128 devices in a mesh: seq: 4 (over z_hi, core), shard: 32 (over y, x, z_lo).
Axes of the slice: x: 4, y: 4, z: 4 (z_hi: 2, z_lo: 2; z = z_hi * 2 + z_lo), core: 2. Of those that a mesh axis runs over, the one named last changes fastest.
Arguments:
- hidden_in: bfloat16 [16384, 1024], P(('seq', 'shard')), may hold values from -6 to 6
- positions: int32 [16384], P(('seq', 'shard')), may hold values from 1 to 16383, as said below
- first_gain: bfloat16 [1024], P('shard'), may hold values from 0.5 to 1.5
- first_shift: bfloat16 [1024], P('shard'), may hold values from -0.5 to 0.5
- second_gain: bfloat16 [1024], P('shard'), may hold values from 0.5 to 1.5
- second_shift: bfloat16 [1024], P('shard'), may hold values from -0.5 to 0.5
- joined_weight: bfloat16 [1024, 3072], P('shard'), may hold values from -0.1875 to 0.1875
- joined_bias: bfloat16 [1024, 3], P('shard'), may hold values from -0.049804688 to 0.049804688
- output_weight: bfloat16 [1024, 1024], P('shard'), may hold values from -0.75 to 0.75
- output_bias: bfloat16 [1024], P('shard'), may hold values from -0.5 to 0.5
- up_weight: bfloat16 [1024, 4096], P('shard'), may hold values from -0.1875 to 0.1875
- up_bias: bfloat16 [4096], P('shard'), may hold values from -0.5 to 0.5
- down_weight: bfloat16 [4096, 1024], P('shard'), may hold values from -0.09375 to 0.09375
- down_bias: bfloat16 [1024], P('shard'), may hold values from -0.5 to 0.5
- cotangent: bfloat16 [16384, 1024], P(('seq', 'shard')), may hold values from -6 to 6
Outputs:
- block_out: bfloat16 [16384, 1024], P(('seq', 'shard'))
- input_grad: bfloat16 [16384, 1024], P(('seq', 'shard'))
- first_gain_grad: float32 [1024], P('shard')
- first_shift_grad: float32 [1024], P('shard')
- second_gain_grad: float32 [1024], P('shard')
- second_shift_grad: float32 [1024], P('shard')
- joined_weight_grad: float32 [1024, 3072], P('shard')
- joined_bias_grad: float32 [1024, 3], P('shard')
- output_weight_grad: float32 [1024, 1024], P('shard')
- output_bias_grad: float32 [1024], P('shard')
- up_weight_grad: float32 [1024, 4096], P('shard')
- up_bias_grad: float32 [4096], P('shard')
- down_weight_grad: float32 [4096, 1024], P('shard')
- down_bias_grad: float32 [1024], P('shard')
Inputs may be any that keep to these rules, and one draw needn't show every extreme that they name: Within each of the 2 sequences of 8192 consecutive tokens the positions rise by 1 or 2 from one token to the next, and the last token of every sequence has position 16383.
All inputs are finite; a program needn't handle non-finite values.
Results may differ from a plain program's by a relative error of at most 0.025.
Values may be sent and summed in bfloat16 or wider, within the bound.
No kernel may reach another device: no remote copies, remote signals or barrier semaphores. Data moves between devices by JAX's collectives and lax.ppermute only.
A program may use at most 256 MiB of HBM per device.

v0:
```python
import jax
import jax.numpy as jnp
from jax import lax
from jax.sharding import PartitionSpec as P

HEAD_DIM = 64
ROTARY = 16


EPS = 1e-05
NEG = -1e30


def normalize(values):
    mean = jnp.mean(values, axis=-1, keepdims=True)
    centered = values - mean
    inverse = lax.rsqrt(jnp.mean(centered * centered, axis=-1, keepdims=True) + EPS)
    return (centered * inverse, inverse)


def rotary_tables(positions):
    inv_freq = 1.0 / 10000.0 ** (jnp.arange(0, ROTARY, 2, dtype=jnp.float32) / ROTARY)
    angles = positions.astype(jnp.float32)[:, None] * inv_freq[None, :]
    angles = jnp.concatenate([angles, angles], axis=1)
    return (jnp.cos(angles), jnp.sin(angles))


def rotate(values, cosine, sine):
    turned = values[..., :ROTARY]
    half = ROTARY // 2
    swapped = jnp.concatenate([-turned[..., half:], turned[..., :half]], axis=-1)
    turned = turned * cosine[:, None, :] + swapped * sine[:, None, :]
    return jnp.concatenate([turned, values[..., ROTARY:]], axis=-1)


def softmax_update(state, query, keys, values, allowed, scale):
    best, total, summed = state
    scores = jnp.einsum("rhd,khd->hrk", query, keys, preferred_element_type=jnp.float32) * scale
    if allowed is not None:
        scores = jnp.where(allowed[None], scores, NEG)
    new_best = jnp.maximum(best, jnp.max(scores, axis=-1))
    weights = jnp.exp(scores - new_best[..., None])
    if allowed is not None:
        weights = jnp.where(allowed[None], weights, 0.0)
    factor = jnp.exp(best - new_best)
    total = total * factor + jnp.sum(weights, axis=-1)
    summed = summed * jnp.transpose(factor)[..., None] + jnp.einsum(
        "hrk,khd->rhd", weights.astype(jnp.bfloat16), values, preferred_element_type=jnp.float32
    )
    return (new_best, total, summed)


def attend_forward(query_heads, key_heads, value_heads, lead, seq_total):
    blocks, rows, wide = query_heads.shape
    heads = wide // HEAD_DIM
    per_seq = blocks // seq_total
    scale = HEAD_DIM ** (-0.5)
    queries = query_heads.reshape(blocks, rows, heads, HEAD_DIM)
    local_pos = lead + jnp.arange(rows, dtype=jnp.int32)

    def fold_step(carry, pieces, start):
        key_piece, value_piece = pieces
        count = key_piece.shape[1]
        key_piece = key_piece.reshape(blocks, count, heads, HEAD_DIM)
        value_piece = value_piece.reshape(blocks, count, heads, HEAD_DIM)
        allowed = jnp.arange(count, dtype=jnp.int32)[None, :] <= local_pos[:, None]
        best, total, summed = carry
        results = []
        for block in range(blocks):
            first = block // per_seq * per_seq
            state = (best[block], total[block], summed[block])
            if block > first:
                state = softmax_update(
                    state,
                    queries[block],
                    key_piece[first:block].reshape(-1, heads, HEAD_DIM),
                    value_piece[first:block].reshape(-1, heads, HEAD_DIM),
                    None,
                    scale,
                )

            def diagonal(inner, block=block):
                return softmax_update(
                    inner, queries[block], key_piece[block], value_piece[block], allowed, scale
                )

            state = lax.cond(start < lead + rows, diagonal, lambda inner: inner, state)
            results.append(state)
        return tuple((jnp.stack([entry[member] for entry in results]) for member in range(3)))

    init = (
        jnp.full((blocks, heads, rows), NEG, jnp.float32),
        jnp.zeros((blocks, heads, rows), jnp.float32),
        jnp.zeros((blocks, rows, heads, HEAD_DIM), jnp.float32),
    )
    best, total, summed = fold_step(
        init,
        (
            lax.all_gather(key_heads, "shard", axis=1, tiled=True),
            lax.all_gather(value_heads, "shard", axis=1, tiled=True),
        ),
        jnp.int32(0),
    )
    log_rows = best + jnp.log(total)
    output = summed / jnp.transpose(total, (0, 2, 1))[..., None]
    return (output.reshape(blocks, rows, wide).astype(jnp.bfloat16), log_rows)


def query_side(grad_query, query, grad_out, log_rows, delta_rows, keys, values, allowed, scale):
    scores = jnp.einsum("rhd,khd->hrk", query, keys, preferred_element_type=jnp.float32) * scale
    probs = jnp.exp(scores - log_rows[..., None])
    if allowed is not None:
        probs = jnp.where(allowed[None], probs, 0.0)
    grad_probs = jnp.einsum("rhd,khd->hrk", grad_out, values, preferred_element_type=jnp.float32)
    grad_scores = (probs * (grad_probs - delta_rows[..., None])).astype(jnp.bfloat16)
    return (
        grad_query
        + jnp.einsum("hrk,khd->rhd", grad_scores, keys, preferred_element_type=jnp.float32) * scale
    )


def key_side(pair, keys, values, queries, grad_outs, log_cols, delta_cols, allowed, scale):
    grad_key, grad_value = pair
    scores = jnp.einsum("khd,qhd->hkq", keys, queries, preferred_element_type=jnp.float32) * scale
    probs = jnp.exp(scores - jnp.transpose(log_cols)[:, None, :])
    if allowed is not None:
        probs = jnp.where(allowed[None], probs, 0.0)
    grad_value = grad_value + jnp.einsum(
        "hkq,qhd->khd", probs.astype(jnp.bfloat16), grad_outs, preferred_element_type=jnp.float32
    )
    grad_probs = jnp.einsum("khd,qhd->hkq", values, grad_outs, preferred_element_type=jnp.float32)
    grad_scores = (probs * (grad_probs - jnp.transpose(delta_cols)[:, None, :])).astype(
        jnp.bfloat16
    )
    grad_key = (
        grad_key
        + jnp.einsum("hkq,qhd->khd", grad_scores, queries, preferred_element_type=jnp.float32)
        * scale
    )
    return (grad_key, grad_value)


def attend_backward(
    query_heads,
    key_heads,
    value_heads,
    grad_heads,
    log_rows,
    delta_local,
    stats_log,
    stats_delta,
    lead,
    seq_total,
):
    blocks, rows, wide = query_heads.shape
    heads = wide // HEAD_DIM
    per_seq = blocks // seq_total
    scale = HEAD_DIM ** (-0.5)
    queries = query_heads.reshape(blocks, rows, heads, HEAD_DIM)
    keys_local = key_heads.reshape(blocks, rows, heads, HEAD_DIM)
    values_local = value_heads.reshape(blocks, rows, heads, HEAD_DIM)
    grads_local = grad_heads.reshape(blocks, rows, heads, HEAD_DIM)
    local_pos = lead + jnp.arange(rows, dtype=jnp.int32)

    def fold_step(carry, pieces, start):
        query_piece, key_piece, value_piece, grad_piece = pieces
        count = query_piece.shape[1]
        query_piece = query_piece.reshape(blocks, count, heads, HEAD_DIM)
        key_piece = key_piece.reshape(blocks, count, heads, HEAD_DIM)
        value_piece = value_piece.reshape(blocks, count, heads, HEAD_DIM)
        grad_piece = grad_piece.reshape(blocks, count, heads, HEAD_DIM)
        remote_pos = jnp.arange(count, dtype=jnp.int32)
        allowed_keys = remote_pos[None, :] <= local_pos[:, None]
        allowed_queries = local_pos[:, None] <= remote_pos[None, :]
        grad_q, grad_k, grad_v = carry
        new_q, new_k, new_v = ([], [], [])
        for block in range(blocks):
            first = block // per_seq * per_seq
            stop = first + per_seq
            current = grad_q[block]
            if block > first:
                current = query_side(
                    current,
                    queries[block],
                    grads_local[block],
                    log_rows[block],
                    delta_local[block],
                    key_piece[first:block].reshape(-1, heads, HEAD_DIM),
                    value_piece[first:block].reshape(-1, heads, HEAD_DIM),
                    None,
                    scale,
                )

            def query_diag(inner, block=block):
                return query_side(
                    inner,
                    queries[block],
                    grads_local[block],
                    log_rows[block],
                    delta_local[block],
                    key_piece[block],
                    value_piece[block],
                    allowed_keys,
                    scale,
                )

            current = lax.cond(start < lead + rows, query_diag, lambda inner: inner, current)
            new_q.append(current)
            pair = (grad_k[block], grad_v[block])
            if block + 1 < stop:
                pair = key_side(
                    pair,
                    keys_local[block],
                    values_local[block],
                    query_piece[block + 1 : stop].reshape(-1, heads, HEAD_DIM),
                    grad_piece[block + 1 : stop].reshape(-1, heads, HEAD_DIM),
                    stats_log[block + 1 : stop].reshape(-1, heads),
                    stats_delta[block + 1 : stop].reshape(-1, heads),
                    None,
                    scale,
                )

            def key_diag(inner, block=block):
                return key_side(
                    inner,
                    keys_local[block],
                    values_local[block],
                    query_piece[block],
                    grad_piece[block],
                    stats_log[block],
                    stats_delta[block],
                    allowed_queries,
                    scale,
                )

            pair = lax.cond(start + count > lead, key_diag, lambda inner: inner, pair)
            new_k.append(pair[0])
            new_v.append(pair[1])
        return (jnp.stack(new_q), jnp.stack(new_k), jnp.stack(new_v))

    zeros = jnp.zeros((blocks, rows, heads, HEAD_DIM), jnp.float32)
    grad_q, grad_k, grad_v = fold_step(
        (zeros, zeros, zeros),
        (
            lax.all_gather(query_heads, "shard", axis=1, tiled=True),
            lax.all_gather(key_heads, "shard", axis=1, tiled=True),
            lax.all_gather(value_heads, "shard", axis=1, tiled=True),
            lax.all_gather(grad_heads, "shard", axis=1, tiled=True),
        ),
        jnp.int32(0),
    )
    return (
        grad_q.reshape(blocks, rows, wide),
        grad_k.reshape(blocks, rows, wide),
        grad_v.reshape(blocks, rows, wide),
    )


def per_device(
    hidden_in,
    positions,
    first_gain,
    first_shift,
    second_gain,
    second_shift,
    joined_weight,
    joined_bias,
    output_weight,
    output_bias,
    up_weight,
    up_bias,
    down_weight,
    down_bias,
    cotangent,
):
    rows, width = hidden_in.shape
    hidden_width = up_weight.shape[1]
    shard_rows = joined_weight.shape[0]
    heads_all = width // HEAD_DIM
    seq_total = lax.axis_size("seq") // 2
    shard_index = lax.axis_index("shard")
    lead = shard_index * rows
    inputs = hidden_in.astype(jnp.float32)
    grad_out = cotangent.astype(jnp.float32)
    scaled, inverse = normalize(inputs)
    cosine, sine = rotary_tables(positions)
    w_joined = lax.all_gather(joined_weight, "shard", axis=0, tiled=True)
    w_up = lax.all_gather(up_weight, "shard", axis=0, tiled=True)
    w_out = lax.all_gather(output_weight, "shard", axis=0, tiled=True)
    gain_a = lax.all_gather(first_gain, "shard", axis=0, tiled=True)
    shift_a = lax.all_gather(first_shift, "shard", axis=0, tiled=True)
    gain_b = lax.all_gather(second_gain, "shard", axis=0, tiled=True)
    shift_b = lax.all_gather(second_shift, "shard", axis=0, tiled=True)
    bias_joined = lax.all_gather(joined_bias, "shard", axis=0, tiled=True)
    front_bias_out = lax.all_gather(output_bias, "shard", axis=0, tiled=True)
    front_bias_down = lax.all_gather(down_bias, "shard", axis=0, tiled=True)
    first_cols = (scaled * gain_a.astype(jnp.float32) + shift_a.astype(jnp.float32)).astype(
        jnp.bfloat16
    )
    second_cols = (scaled * gain_b.astype(jnp.float32) + shift_b.astype(jnp.float32)).astype(
        jnp.bfloat16
    )
    joined_sum = jnp.dot(first_cols, w_joined, preferred_element_type=jnp.float32)
    front_up_sum = jnp.dot(second_cols, w_up, preferred_element_type=jnp.float32)
    small = jnp.concatenate(
        [
            jnp.stack([gain_a, shift_a, gain_b, shift_b, front_bias_out, front_bias_down], axis=1),
            bias_joined,
        ],
        axis=1,
    ).astype(jnp.float32)
    table = small
    joined_sum, up_sum, out_full, table = (joined_sum, front_up_sum, w_out, table)
    gain_one = table[:, 0]
    shift_one = table[:, 1]
    gain_two = table[:, 2]
    shift_two = table[:, 3]
    bias_out = table[:, 4]
    bias_down = table[:, 5]
    joined = joined_sum + jnp.transpose(table[:, 6:9]).reshape(-1)
    joined_heads = joined.reshape(rows, 3, heads_all, HEAD_DIM)
    query_turned = rotate(joined_heads[:, 0], cosine, sine)
    key_turned = rotate(joined_heads[:, 1], cosine, sine)
    stacked = (
        jnp.stack([query_turned, key_turned, joined_heads[:, 2]], axis=1)
        .reshape(1, rows, 3, width)
        .astype(jnp.bfloat16)
    )
    regrouped = lax.all_to_all(stacked, "seq", split_axis=3, concat_axis=0, tiled=True)
    query_heads = regrouped[:, :, 0]
    key_heads = regrouped[:, :, 1]
    value_heads = regrouped[:, :, 2]
    out_heads, log_rows = attend_forward(query_heads, key_heads, value_heads, lead, seq_total)
    returned = lax.all_to_all(out_heads, "seq", split_axis=0, concat_axis=2, tiled=True)
    attention_mixed_tok = returned.reshape(rows, width)
    attention = (
        jnp.dot(attention_mixed_tok, out_full, preferred_element_type=jnp.float32) + bias_out
    )
    query_heads, key_heads, value_heads, out_heads, log_rows, mixed_tok, attention = (
        query_heads,
        key_heads,
        value_heads,
        out_heads,
        log_rows,
        attention_mixed_tok,
        attention,
    )
    w_down = lax.all_gather(down_weight, "shard", axis=0, tiled=True)
    bias_up = lax.all_gather(up_bias, "shard", axis=0, tiled=True)
    bias_piece = bias_up.astype(jnp.float32)
    pre = up_sum + bias_piece
    act = jax.nn.gelu(pre, approximate=False).astype(jnp.bfloat16)
    mixed_sum = jnp.dot(act, w_down, preferred_element_type=jnp.float32)
    bias_full = bias_piece
    back = jnp.einsum("rd,fd->rf", cotangent, w_down, preferred_element_type=jnp.float32)
    grad_hidden = back
    mixed_sum, bias_full, feed_activated, grad_hidden = (mixed_sum, bias_full, act, grad_hidden)
    feed, up_pre, activated, grad_hidden = (
        mixed_sum + bias_down,
        up_sum + bias_full,
        feed_activated,
        grad_hidden,
    )
    block_out = (inputs + attention + feed).astype(jnp.bfloat16)
    _, gelu_pull = jax.vjp(lambda value: jax.nn.gelu(value, approximate=False), up_pre)
    grad_up = gelu_pull(grad_hidden)[0].astype(jnp.bfloat16)
    grad_mixed = jnp.einsum(
        "rd,fd->rf", cotangent, out_full, preferred_element_type=jnp.float32
    ).astype(jnp.bfloat16)
    grad_heads = lax.all_to_all(
        grad_mixed.reshape(1, rows, width), "seq", split_axis=2, concat_axis=0, tiled=True
    )
    blocks, head_rows, wide = out_heads.shape
    heads = wide // HEAD_DIM
    delta_t = jnp.sum(
        (grad_heads.astype(jnp.float32) * out_heads.astype(jnp.float32)).reshape(
            blocks, head_rows, heads, HEAD_DIM
        ),
        axis=-1,
    )
    log_t = jnp.transpose(log_rows, (0, 2, 1))
    stats_log, stats_delta = (
        lax.all_gather(log_t, "shard", axis=1, tiled=True),
        lax.all_gather(delta_t, "shard", axis=1, tiled=True),
    )
    delta_local = jnp.transpose(delta_t, (0, 2, 1))
    grad_q, grad_k, grad_v = attend_backward(
        query_heads,
        key_heads,
        value_heads,
        grad_heads,
        log_rows,
        delta_local,
        stats_log,
        stats_delta,
        lead,
        seq_total,
    )
    stacked_grads = jnp.stack([grad_q, grad_k, grad_v], axis=2).astype(jnp.bfloat16)
    returned_grads = lax.all_to_all(stacked_grads, "seq", split_axis=0, concat_axis=3, tiled=True)
    grad_turned = returned_grads.reshape(rows, 3, heads_all, HEAD_DIM).astype(jnp.float32)
    _, rotate_pull = jax.vjp(lambda value: rotate(value, cosine, sine), query_turned)
    grad_joined = (
        jnp.stack(
            [
                rotate_pull(grad_turned[:, 0])[0],
                rotate_pull(grad_turned[:, 1])[0],
                grad_turned[:, 2],
            ],
            axis=1,
        )
        .reshape(rows, 3 * width)
        .astype(jnp.bfloat16)
    )
    w_joined = lax.all_gather(joined_weight, "shard", axis=0, tiled=True)
    w_up = lax.all_gather(up_weight, "shard", axis=0, tiled=True)
    part_first = jnp.einsum("rc,fc->rf", grad_joined, w_joined, preferred_element_type=jnp.float32)
    part_second = jnp.einsum("rc,fc->rf", grad_up, w_up, preferred_element_type=jnp.float32)
    grad_first = part_first
    grad_second = part_second
    grad_first, grad_second = (grad_first, grad_second)
    grad_scaled = grad_first * gain_one + grad_second * gain_two
    mean_plain = jnp.mean(grad_scaled, axis=-1, keepdims=True)
    mean_scaled = jnp.mean(grad_scaled * scaled, axis=-1, keepdims=True)
    input_grad = (grad_out + inverse * (grad_scaled - mean_plain - scaled * mean_scaled)).astype(
        jnp.bfloat16
    )
    totals = (
        jnp.sum(grad_first * scaled, axis=0),
        jnp.sum(grad_first, axis=0),
        jnp.sum(grad_second * scaled, axis=0),
        jnp.sum(grad_second, axis=0),
        jnp.sum(grad_joined.astype(jnp.float32), axis=0),
        jnp.sum(grad_out, axis=0),
        jnp.sum(grad_up.astype(jnp.float32), axis=0),
    )
    summed = lax.psum(
        (totals[0], totals[1], totals[2], totals[3], totals[4], totals[5], totals[6]),
        ("seq", "shard"),
    )
    row_start = shard_index * shard_rows
    wide_rows = up_bias.shape[0]

    def own_rows(vector):
        return lax.dynamic_slice_in_dim(vector, row_start, shard_rows, 0)

    first_gain_grad = own_rows(summed[0])
    first_shift_grad = own_rows(summed[1])
    second_gain_grad = own_rows(summed[2])
    second_shift_grad = own_rows(summed[3])
    joined_bias_grad = own_rows(jnp.transpose(summed[4].reshape(3, width)))
    output_bias_grad = own_rows(summed[5])
    up_bias_grad = lax.dynamic_slice_in_dim(summed[6], shard_index * wide_rows, wide_rows, 0)
    first_full = (scaled * gain_one + shift_one).astype(jnp.bfloat16)
    second_full = (scaled * gain_two + shift_two).astype(jnp.bfloat16)
    first_cols = first_full
    second_cols = second_full
    front_part = lax.psum_scatter(
        jnp.concatenate(
            [
                jnp.einsum(
                    "rf,rc->fc", first_cols, grad_joined, preferred_element_type=jnp.float32
                ),
                jnp.einsum("rf,rc->fc", second_cols, grad_up, preferred_element_type=jnp.float32),
                jnp.einsum("rf,rc->fc", mixed_tok, cotangent, preferred_element_type=jnp.float32),
            ],
            axis=1,
        ).astype(jnp.bfloat16),
        "shard",
        scatter_dimension=0,
        tiled=True,
    ).astype(jnp.float32)
    down_part = lax.psum_scatter(
        jnp.einsum("rf,rd->fd", activated, cotangent, preferred_element_type=jnp.float32).astype(
            jnp.bfloat16
        ),
        "shard",
        scatter_dimension=0,
        tiled=True,
    ).astype(jnp.float32)
    front_part, down_part = (
        lax.psum(front_part.astype(jnp.bfloat16), "seq").astype(jnp.float32),
        lax.psum(down_part.astype(jnp.bfloat16), "seq").astype(jnp.float32),
    )
    joined_weight_grad = front_part[:, : 3 * width]
    up_weight_grad = front_part[:, 3 * width : 3 * width + hidden_width]
    output_weight_grad = front_part[:, 3 * width + hidden_width :]
    return (
        block_out,
        input_grad,
        first_gain_grad,
        first_shift_grad,
        second_gain_grad,
        second_shift_grad,
        joined_weight_grad,
        joined_bias_grad,
        output_weight_grad,
        output_bias_grad,
        up_weight_grad,
        up_bias_grad,
        down_part,
        output_bias_grad,
    )


def solution(mesh):
    in_specs = (
        P(("seq", "shard"), None),
        P(("seq", "shard")),
        P("shard"),
        P("shard"),
        P("shard"),
        P("shard"),
        P("shard", None),
        P("shard", None),
        P("shard", None),
        P("shard"),
        P("shard", None),
        P("shard"),
        P("shard", None),
        P("shard"),
        P(("seq", "shard"), None),
    )
    out_specs = (
        P(("seq", "shard"), None),
        P(("seq", "shard"), None),
        P("shard"),
        P("shard"),
        P("shard"),
        P("shard"),
        P("shard", None),
        P("shard", None),
        P("shard", None),
        P("shard"),
        P("shard", None),
        P("shard"),
        P("shard", None),
        P("shard"),
    )
    return jax.shard_map(
        per_device, mesh=mesh, in_specs=in_specs, out_specs=out_specs, check_vma=False
    )
```

profile of v0, /device:TPU:1, one launch (start us, length us, event | category | flops | bytes accessed | tf_op | source)
XLA Modules:
  0.0 2378.2 jit_solution(1747658654512687701)
XLA Ops:
  10.0 135.1 %all-gather.17.cloned.1.call-done = bf16[1024,1024]{1,0:T(8,128)(2,1)} async-done(((bf16[32,1024]{1,0:T(8,128)(2,1)}), bf16[1024,1024]{1,0:T(8,128)(2,1)}) %all-gather.17.cloned.1.call-update) | async-done | bytes 2097168 | tf_op jit(solution)/shard_map/all_gather | solution.py:289
  150.9 39.3 %all_to_all.60 = bf16[4,2,16384]{2,1,0:T(2,128)(2,1)S(1)} all-to-all(bf16[4,2,16384]{2,1,0:T(2,128)(2,1)S(1)} %reshape.651), channel_id=1, replica_groups=mesh['seq'=4,'shard'=32] {'seq'}, dimensions={0} | all-to-all | bytes 524288 | tf_op jit(solution)/shard_map/all_to_all | solution.py:370
  198.2 136.3 %all-reduce.15 = (bf16[1024]{0:T(1024)(128)(2,1)S(1)}, bf16[1024]{0:T(1024)(128)(2,1)S(1)}, bf16[1024]{0:T(1024)(128)(2,1)S(1)}, bf16[1024]{0:T(1024)(128)(2,1)S...) all-reduce(bf16[1024]{0:T(1024)(128)(2,1)S(1)} %dynamic-update-slic, ...), channel_id=1, replica_groups=mesh['seq'=4,'shard'=32] {'shard'}, use_global_device_ids=true, to_apply=%add.11 | all-reduce | flops 6144 | bytes 24576
  334.6 64.3 %all-gather.4 = bf16[32,32,3]{1,2,0:T(4,128)(2,1)S(1)} all-gather(bf16[1,32,3]{1,2,0:T(4,128)(2,1)} %bitcast.786), channel_id=1, replica_groups=mesh['seq'=4,'shard'=32] {'shard'}, dimensions={0}, use_global_device_ids=true | all-gather | bytes 6336 | tf_op jit(solution)/shard_map/all_gather | solution.py:294
  409.4 76.8 %all_to_all.61 = bf16[1,128,3,1024]{1,2,0,3:T(4,128)(2,1)S(1)} all-to-all(bf16[1,128,3,1024]{1,2,0,3:T(4,128)(2,1)S(1)} %copy.91), channel_id=1, replica_groups=mesh['seq'=4,'shard'=32] {'seq'}, dimensions={3} | all-to-all | bytes 1572864 | tf_op jit(solution)/shard_map/all_to_all | solution.py:329
  488.8 65.8 %all-gather.5 = bf16[32,1,128]{2,1,0:T(2,128)(2,1)S(1)} all-gather(bf16[1,1,128]{2,1,0:T(2,128)(2,1)S(1)} %bitcast.787), channel_id=1, replica_groups=mesh['seq'=4,'shard'=32] {'shard'}, dimensions={0}, use_global_device_ids=true | all-gather | bytes 8448 | tf_op jit(solution)/shard_map/all_gather | solution.py:349
  563.6 162.2 %all-gather.21.cloned.1.call-done = bf16[4096,1024]{1,0:T(8,128)(2,1)} async-done(((bf16[128,1024]{1,0:T(8,128)(2,1)}), bf16[4096,1024]{1,0:T(8,128)(2,1)}) %all-gather.21.cloned.1.call-update) | async-done | bytes 8388624 | tf_op jit(solution)/shard_map/all_gather | solution.py:348
  725.9 11.0 convert_reduce_fusion
  743.9 206.0 %all-gather.29.cloned.1.call-done = bf16[4,1,4096,256]{2,3,0,1:T(8,128)(2,1)} async-done(((bf16[4,1,128,256]{2,3,0,1:T(8,128)(2,1)}), bf16[4,1,4096,256]{2,3,0,1:T(8,128)(2,1)}) %all-gather.29.cloned.1.call-update) | async-done | bytes 8388624 | tf_op jit(solution)/shard_map/all_gather | solution.py:248
  954.6 234.8 %all-gather.23.cloned.1.call-done = bf16[4,4096,1,256]{1,3,0,2:T(8,128)(2,1)} async-done(((bf16[4,128,1,256]{1,3,0,2:T(8,128)(2,1)}), bf16[4,4096,1,256]{1,3,0,2:T(8,128)(2,1)}) %all-gather.23.cloned.1.call-update) | async-done | bytes 8388624 | tf_op jit(solution)/shard_map/all_gather | solution.py:99
  1200.3 223.9 %all-gather.25.cloned.1.call-done = bf16[4,4096,1,256]{1,3,0,2:T(8,128)(2,1)} async-done(((bf16[4,128,1,256]{1,3,0,2:T(8,128)(2,1)}), bf16[4,4096,1,256]{1,3,0,2:T(8,128)(2,1)}) %all-gather.25.cloned.1.call-update) | async-done | bytes 8388624 | tf_op jit(solution)/shard_map/all_gather | solution.py:100
  1438.3 11.6 conditional.12
  1450.6 12.0 conditional.14
  1463.2 10.1 conditional.13
  1474.0 10.1 conditional.15
  1488.2 74.6 %all_gather.73 = f32[4,4096,4]{1,2,0:T(4,128)S(1)} all-gather(f32[4,128,4]{1,2,0:T(4,128)S(1)} %fusion.586), channel_id=1, replica_groups=mesh['seq'=4,'shard'=32] {'shard'}, dimensions={1}, use_global_device_ids=true | all-gather | bytes 270336 | tf_op jit(solution)/shard_map/all_gather | solution.py:383
  1564.0 73.9 %all_gather.75 = f32[4,4096,4]{1,2,0:T(4,128)} all-gather(f32[4,128,4]{1,2,0:T(4,128)S(1)} %multiply_reduce_fusion.2), channel_id=1, replica_groups=mesh['seq'=4,'shard'=32] {'shard'}, dimensions={1}, use_global_device_ids=true | all-gather | bytes 270336 | tf_op jit(solution)/shard_map/all_gather | solution.py:384
  1638.0 41.2 %all-gather.27.cloned.1.call-done = bf16[4,4096,1,256]{1,3,0,2:T(8,128)(2,1)} async-done(((bf16[4,128,1,256]{1,3,0,2:T(8,128)(2,1)}), bf16[4,4096,1,256]{1,3,0,2:T(8,128)(2,1)}) %all-gather.27.cloned.1.call-update) | async-done | bytes 8388624 | tf_op jit(solution)/shard_map/all_gather | solution.py:245
  1690.8 8.9 fusion.447
  1708.4 9.0 fusion.445
  1727.2 15.1 conditional.17
  1742.9 15.0 conditional.16
  1758.6 16.2 conditional.18
  1783.1 16.4 conditional.19
  1790.1 8.8 fusion.153
  1800.5 20.5 conditional.21
  1821.7 20.4 conditional.23
  1843.9 16.6 all-to-all-start.1
  1861.5 20.4 conditional.20
  1882.0 20.5 conditional.22
  1951.9 339.6 %reduce-scatter.3.cloned.1.call-done = bf16[32,8192]{1,0:T(8,128)(2,1)} async-done(((bf16[1024,8192]{1,0:T(8,128)(2,1)}), bf16[32,8192]{1,0:T(8,128)(2,1)}) %reduce-scatter.3.cloned.1.call-update) | async-done | bytes 524304 | tf_op jit(solution)/shard_map/reduce_scatter | solution.py:458
  2292.6 67.7 %all-reduce.14 = (f32[1024]{0:T(1024)S(1)}, f32[1024]{0:T(1024)S(1)}, f32[1024]{0:T(1024)S(1)}, f32[1024]{0:T(1024)S(1)}, f32[3,1024]{1,0:T(4,128)S(1)}, /*index=5*/f32[1024]{0:T(1024)S(1)}, f32[4096]{0:T(1024)S(1)}) all-reduce(f32[1024]{0:T(1024)S(1)} %get-tuple-element.754, ...), channel_id=1, replica_groups=mesh['seq'=4,'shard'=32] {'seq','shard'}, use_global_device_ids=true, to_apply=%region_42.43 | all-reduce | flops 12288 | bytes 98304 | tf_op jit(solution)/shard_map/psum | solution.py:437
  (415 shorter events, 365.6 us)
Async XLA Ops:
  7.2 392.8 %copy-start.5 = (bf16[128,1024]{1,0:T(8,128)(2,1)S(1)}, bf16[128,1024]{1,0:T(8,128)(2,1)}, u32[]{:S(2)}) copy-start(bf16[128,1024]{1,0:T(8,128)(2,1)} %param.39) | copy-start | bytes 786436
  7.2 138.0 %all-gather.17.cloned.1.call-start = ((), (), s32[]{:S(2)}) async-start(), calls=%async_computation.7 | async-start | bytes 2162688 | tf_op jit(solution)/shard_map/all_gather | solution.py:289
  7.9 392.5 %all-gather.15.cloned.1.call-start = ((), (), s32[]{:S(2)}) async-start(), calls=%async_computation.6 | async-start | bytes 6488064 | tf_op jit(solution)/shard_map/all_gather | solution.py:287
  8.7 550.1 %all-gather.19.cloned.1.call-start = ((), (), s32[]{:S(2)}) async-start(), calls=%async_computation.8 | async-start | bytes 8650752 | tf_op jit(solution)/shard_map/all_gather | solution.py:288
  9.4 716.5 %all-gather.21.cloned.1.call-start = ((), (), s32[]{:S(2)}) async-start(), calls=%async_computation.9 | async-start | bytes 8650752 | tf_op jit(solution)/shard_map/all_gather | solution.py:348
  10.0 939.9 %all-gather.29.cloned.1.call-start = ((), (), s32[]{:S(2)}) async-start(), calls=%async_computation.15 | async-start | bytes 8650752 | tf_op jit(solution)/shard_map/all_gather | solution.py:248
  191.2 998.2 %all-gather.23.cloned.1.call-start = ((), (), s32[]{:S(2)}) async-start(), calls=%async_computation.12 | async-start | bytes 8650752 | tf_op jit(solution)/shard_map/all_gather | solution.py:99
  400.1 158.7 %copy-start.73 = (f32[128]{0:T(128)}, f32[128]{0:T(128)S(1)}, u32[]{:S(2)}) copy-start(f32[128]{0:T(128)S(1)} %broadcast_multiply_fusion.3) | copy-start | bytes 1540
  400.4 158.4 %copy-start.75 = (f32[128]{0:T(128)}, f32[128]{0:T(128)S(1)}, u32[]{:S(2)}) copy-start(f32[128]{0:T(128)S(1)} %add_rsqrt_fusion) | copy-start | bytes 1540
  405.9 82.8 %copy-start.93 = (bf16[128]{0:T(256)(128)(2,1)S(1)}, bf16[128]{0:T(256)(128)(2,1)}, u32[]{:S(2)}) copy-start(bf16[128]{0:T(256)(128)(2,1)} %param.50) | copy-start | bytes 772
  405.9 151.4 %copy-start.23 = (bf16[1,128,1024]{1,2,0:T(8,128)(2,1)S(1)}, bf16[1,128,1024]{1,2,0:T(8,128)(2,1)}, u32[]{:S(2)}) copy-start(bf16[1,128,1024]{1,2,0:T(8,128)(2,1)} %copy.97) | copy-start | bytes 786436
  487.2 936.9 %all-gather.25.cloned.1.call-start = ((), (), s32[]{:S(2)}) async-start(), calls=%async_computation.13 | async-start | bytes 8650752 | tf_op jit(solution)/shard_map/all_gather | solution.py:100
  487.9 1191.2 %all-gather.27.cloned.1.call-start = ((), (), s32[]{:S(2)}) async-start(), calls=%async_computation.14 | async-start | bytes 8650752 | tf_op jit(solution)/shard_map/all_gather | solution.py:245
  488.7 1463.2 %reduce-scatter.5.cloned.1.call-start = ((), (), s32[]{:S(2)}) async-start(), calls=%async_computation.11 | async-start | bytes 8650752 | tf_op jit(solution)/shard_map/reduce_scatter | solution.py:473
  555.9 170.0 %copy-start.20 = (bf16[128,1024]{1,0:T(8,128)(2,1)S(1)}, bf16[128,1024]{1,0:T(8,128)(2,1)}, u32[]{:S(2)}) copy-start(bf16[128,1024]{1,0:T(8,128)(2,1)} %param.53) | copy-start | bytes 786436
  1484.8 78.0 %copy-start.61 = (f32[1,4,128]{2,1,0:T(4,128)}, f32[1,4,128]{2,1,0:T(4,128)S(1)}, u32[]{:S(2)}) copy-start(f32[1,4,128]{2,1,0:T(4,128)S(1)} %get-tuple-element.543) | copy-start | bytes 6148
  1562.8 121.7 %copy-start.29 = (f32[4,4096,4]{1,2,0:T(4,128)}, f32[4,4096,4]{1,2,0:T(4,128)S(1)}, u32[]{:S(2)}) copy-start(f32[4,4096,4]{1,2,0:T(4,128)S(1)} %all_gather.73) | copy-start | bytes 786436
  1717.5 25.4 %copy-start.77 = (f32[4,4,128]{2,1,0:T(4,128)}, f32[4,4,128]{2,1,0:T(4,128)S(1)}, u32[]{:S(2)}) copy-start(f32[4,4,128]{2,1,0:T(4,128)S(1)} %maximum_add_fusion) | copy-start | bytes 24580
  1821.1 22.8 copy-start.34
  1821.1 22.8 copy-start.37
  1843.9 60.6 %all-to-all-start.1 = ((bf16[4,128,256]{1,2,0:T(8,128)(2,1)}), bf16[4,128,256]{1,2,0:T(8,128)(2,1)S(1)}, u32[]{:S(2)}, u32[]{:S(2)}) async-start(bf16[4,128,256]{1,2,0:T(8,128)(2,1)} %fusion.483), calls=%async_computation.1 | async-start | bytes 524288 | tf_op jit(solution)/shard_map/all_to_all | solution.py:334
  1881.9 27.7 %copy-start.6 = (bf16[128,1024]{1,0:T(8,128)(2,1)S(1)}, bf16[128,1024]{1,0:T(8,128)(2,1)}, u32[]{:S(2)}) copy-start(bf16[128,1024]{1,0:T(8,128)(2,1)} %param.39) | copy-start | bytes 786436
  1881.9 27.7 %copy-start.18 = (bf16[128,4096]{1,0:T(8,128)(2,1)S(1)}, bf16[128,4096]{1,0:T(8,128)(2,1)}, u32[]{:S(2)}) copy-start(bf16[128,4096]{1,0:T(8,128)(2,1)} %get-tuple-element.706) | copy-start | bytes 3145732
  1881.9 27.7 %copy-start.56 = (f32[1024,1]{0,1:T(1,128)S(1)}, f32[1024,1]{0,1:T(1,128)}, u32[]{:S(2)}) copy-start(f32[1024,1]{0,1:T(1,128)} %get-tuple-element.784) | copy-start | bytes 12292
  1881.9 27.7 %copy-start.60 = (f32[1024,1]{0,1:T(1,128)S(1)}, f32[1024,1]{0,1:T(1,128)}, u32[]{:S(2)}) copy-start(f32[1024,1]{0,1:T(1,128)} %get-tuple-element.782) | copy-start | bytes 12292
  1882.0 27.7 %copy-start.74 = (f32[128]{0:T(128)S(1)}, f32[128]{0:T(128)}, u32[]{:S(2)}) copy-start(f32[128]{0:T(128)} %copy-done.73) | copy-start | bytes 1540
  1882.0 27.7 %copy-start.76 = (f32[128]{0:T(128)S(1)}, f32[128]{0:T(128)}, u32[]{:S(2)}) copy-start(f32[128]{0:T(128)} %copy-done.75) | copy-start | bytes 1540
  1904.5 17.1 all-to-all-start.3
  1909.3 382.2 %reduce-scatter.3.cloned.1.call-start = ((), (), s32[]{:S(2)}) async-start(), calls=%async_computation.10 | async-start | bytes 17301504 | tf_op jit(solution)/shard_map/reduce_scatter | solution.py:458
  1932.7 431.2 %all-reduce.19.cloned.1.call-start = ((), (), s32[]{:S(2)}) async-start(), calls=%async_computation.16 | async-start | bytes 1572864 | tf_op jit(solution)/shard_map/psum | solution.py:482
  1939.9 351.7 %copy-start.22 = (bf16[128,1024]{1,0:T(8,128)(2,1)S(1)}, bf16[128,1024]{1,0:T(8,128)(2,1)}, u32[]{:S(2)}) copy-start(bf16[128,1024]{1,0:T(8,128)(2,1)} %param.53) | copy-start | bytes 786436
  1939.9 352.7 %copy-start.88 = (f32[4096]{0:T(1024)S(1)}, f32[4096]{0:T(1024)}, u32[]{:S(2)}) copy-start(f32[4096]{0:T(1024)} %get-tuple-element.705) | copy-start | bytes 49156
  (78 other events, 589.7 us)
Sparse Core Ops, SparseCore 0:
  9.7 135.4 all-gather.16
  146.8 170.4 all-gather.14
  318.9 216.9 all-gather.18
  537.4 188.4 all-gather.20
  727.9 222.0 all-gather.28
  951.9 237.4 all-gather.22
  1191.6 232.4 all-gather.24
  1426.2 252.8 all-gather.26
  1681.5 201.0 reduce-scatter.4
  1932.8 358.6 reduce-scatter.2
  2294.1 45.1 all-reduce.18
where the time goes:
time: 2390 us; the launch traced here: 2380 us
  waiting for transfers between devices  1350 us (56%)
  blocking collectives  599 us (25%)
  matrix products  279 us (12%)
  local copies, waits for them, and re-layouts  71.7 us (3%)
  other arithmetic  38.7 us (2%)
    reduce_scatter x1, waiting for transfers between devices, per_device(): lax.psum_scatter(jnp.concatenate([jnp.einsum('rf,rc->fc', first_cols, gra...  340 us
    all_gather x1, waiting for transfers between devices, attend_forward(): lax.all_gather(key_heads, 'shard', axis=1, tiled=True)  235 us
    all_gather x1, waiting for transfers between devices, attend_forward(): lax.all_gather(value_heads, 'shard', axis=1, tiled=True)  224 us
    all_gather x1, waiting for transfers between devices, attend_backward(): lax.all_gather(grad_heads, 'shard', axis=1, tiled=True)  206 us
    all_gather x1, waiting for transfers between devices, per_device(): w_down = lax.all_gather(down_weight, 'shard', axis=0, tiled=True)  162 us
    unnamed x1, blocking collectives  136 us
    all_gather x1, waiting for transfers between devices, per_device(): w_out = lax.all_gather(output_weight, 'shard', axis=0, tiled=True)  135 us
    all_to_all x1, blocking collectives, per_device(): lax.all_to_all(stacked, 'seq', split_axis=3, concat_axis=0, tiled=True)  76.8 us
  transfers between devices with their start and end apart: 13, of which 8 were waited for; matrix products, arithmetic and copies ran while one was open for 15% of the time, Pallas kernels for 0%

commit v1 on v0

v1 whole, which is shorter than its diff:
```python
import jax
import jax.numpy as jnp
import numpy as np
from jax import lax
from jax.experimental import pallas as pl
from jax.experimental.pallas import tpu as pltpu
from jax.sharding import Mesh
from jax.sharding import PartitionSpec as P

HEAD_DIM = 64
ROTARY = 16
EPS = 1e-05
NEG = -1e30
HIGH = lax.Precision.HIGHEST
MIDDLE = lax.Precision.HIGH
BF = jnp.bfloat16
F32 = jnp.float32
ROW = 128
QT = 512
KT = 512
AXES = ("zh", "c", "y", "x", "zl")
PLANE = ("x", "zl")
SHARD = ("y", "x", "zl")


def attention_kernel(which, msg, out, kv, kvt, qg, qz, gz, dkv):
    sources, blocks = msg.shape[0], msg.shape[1]
    chunks = blocks - 2
    span = sources * ROW
    low_rows = lax.broadcasted_iota(jnp.int32, (2 * HEAD_DIM, ROW), 0) < HEAD_DIM
    low_lanes = lax.broadcasted_iota(jnp.int32, (ROW, 2 * HEAD_DIM), 1) < HEAD_DIM

    def key_place(source, place):
        chunk = lax.rem(place + which[1] * (chunks // 2), chunks)
        return pl.multiple_of(chunk * span + source * ROW, ROW)

    def load_keys(index, carry):
        source, place = index // chunks, index % chunks
        at = key_place(source, place)
        block = msg[source, place]
        kv[pl.ds(at, ROW), :] = block
        kvt[:, pl.ds(at, ROW)] = block.astype(F32).T.astype(BF)
        dkv[pl.ds(at, ROW), :] = jnp.zeros((ROW, 2 * HEAD_DIM), F32)
        return carry

    lax.fori_loop(0, sources * chunks, load_keys, 0)

    def load_queries(index, carry):
        source, part = index // 2, index % 2
        at = pl.multiple_of(part * span + source * ROW, ROW)
        block = msg[source, chunks + part].astype(F32)
        block = jnp.where(low_lanes, block * (HEAD_DIM**-0.5), block)
        qg[pl.ds(at, ROW), :] = block.astype(BF)
        turned = block.T
        qz[:, pl.ds(at, ROW)] = jnp.where(low_rows, turned, 0.0).astype(BF)
        gz[:, pl.ds(at, ROW)] = jnp.where(low_rows, 0.0, turned).astype(BF)
        return carry

    lax.fori_loop(0, sources * 2, load_queries, 0)
    tiles = span // QT
    lanes_tile = lax.broadcasted_iota(jnp.int32, (QT, 2 * HEAD_DIM), 1) < HEAD_DIM
    causal = lax.broadcasted_iota(jnp.int32, (KT, QT), 0) <= lax.broadcasted_iota(
        jnp.int32, (KT, QT), 1
    )

    def one_tile(index, carry):
        part, tile = index // tiles, index % tiles
        chunk = jnp.where(part == which[1], which[0], chunks - 1 - which[0])
        at = pl.multiple_of(index * QT, QT)
        full = chunk * (span // KT) + tile
        query_t = qz[:, pl.ds(at, QT)]
        grad_t = gz[:, pl.ds(at, QT)]

        def forward(step, state, masked):
            best, total, summed = state
            k_at = pl.multiple_of(step * KT, KT)
            scores = jnp.dot(kv[pl.ds(k_at, KT), :], query_t, preferred_element_type=F32)
            if masked:
                scores = jnp.where(causal, scores, NEG)
            new_best = jnp.maximum(best, jnp.max(scores, axis=0, keepdims=True))
            probs = jnp.exp(scores - new_best)
            factor = jnp.exp(best - new_best)
            total = total * factor + jnp.sum(probs, axis=0, keepdims=True)
            summed = summed * factor + jnp.dot(
                kvt[HEAD_DIM:, pl.ds(k_at, KT)], probs.astype(BF), preferred_element_type=F32
            )
            return new_best, total, summed

        state = (
            jnp.full((1, QT), NEG, F32),
            jnp.zeros((1, QT), F32),
            jnp.zeros((HEAD_DIM, QT), F32),
        )
        state = lax.fori_loop(0, full, lambda s, v: forward(s, v, False), state)
        best, total, summed = forward(full, state, True)
        mixed = (summed / total).astype(BF).astype(F32)
        log_rows = best + jnp.log(total)
        delta = jnp.sum(mixed * grad_t[HEAD_DIM:, :].astype(F32), axis=0, keepdims=True)
        both = qg[pl.ds(at, QT), :]
        zero = jnp.zeros_like(both)
        only_query = jnp.where(lanes_tile, both, zero)
        only_grad = jnp.where(lanes_tile, zero, both)

        def backward(step, grad_query, masked):
            k_at = pl.multiple_of(step * KT, KT)
            block = kv[pl.ds(k_at, KT), :]
            scores = jnp.dot(block, query_t, preferred_element_type=F32)
            probs = jnp.exp(scores - log_rows)
            if masked:
                probs = jnp.where(causal, probs, 0.0)
            grad_probs = jnp.dot(block, grad_t, preferred_element_type=F32)
            grad_scores = (probs * (grad_probs - delta)).astype(BF)
            dkv[pl.ds(k_at, KT), :] += jnp.dot(
                grad_scores, only_query, preferred_element_type=F32
            ) + jnp.dot(probs.astype(BF), only_grad, preferred_element_type=F32)
            return grad_query + jnp.dot(
                kvt[:HEAD_DIM, pl.ds(k_at, KT)], grad_scores, preferred_element_type=F32
            )

        grad_query = jnp.zeros((HEAD_DIM, QT), F32)
        grad_query = lax.fori_loop(0, full, lambda s, v: backward(s, v, False), grad_query)
        grad_query = backward(full, grad_query, True) * (HEAD_DIM**-0.5)
        result = jnp.concatenate([grad_query, mixed], axis=0).T.astype(BF)
        for piece in range(QT // ROW):
            out[tile * (QT // ROW) + piece, chunks + part] = result[
                piece * ROW : (piece + 1) * ROW
            ]
        return carry

    lax.fori_loop(0, 2 * tiles, one_tile, 0)

    def store_keys(index, carry):
        source, place = index // chunks, index % chunks
        out[source, place] = dkv[pl.ds(key_place(source, place), ROW), :].astype(BF)
        return carry

    lax.fori_loop(0, sources * chunks, store_keys, 0)


def attend(message, which):
    sources, blocks = message.shape[0], message.shape[1]
    keys = sources * (blocks - 2) * ROW
    queries = sources * 2 * ROW
    wide = 2 * HEAD_DIM
    pairs = keys * queries * 9 // 16
    return pl.pallas_call(
        attention_kernel,
        out_shape=jax.ShapeDtypeStruct(message.shape, BF),
        in_specs=[
            pl.BlockSpec(memory_space=pltpu.SMEM),
            pl.BlockSpec(memory_space=pltpu.VMEM),
        ],
        out_specs=pl.BlockSpec(memory_space=pltpu.VMEM),
        scratch_shapes=[
            pltpu.VMEM((keys, wide), BF),
            pltpu.VMEM((wide, keys), BF),
            pltpu.VMEM((queries, wide), BF),
            pltpu.VMEM((wide, queries), BF),
            pltpu.VMEM((wide, queries), BF),
            pltpu.VMEM((keys, wide), F32),
        ],
        compiler_params=pltpu.CompilerParams(vmem_limit_bytes=48 * 1024 * 1024),
        cost_estimate=pl.CostEstimate(
            flops=pairs * 14 * HEAD_DIM,
            bytes_accessed=4 * sources * blocks * ROW * wide,
            transcendentals=2 * pairs,
        ),
        name="attention",
    )(which, message)


def front_kernel(
    which, own, far, table, bias, cosine, sine, w_joined, w_out, msg, first, second, scaled, grads
):
    step = pl.program_id(0)
    steps = pl.num_programs(0)
    rows = 2 * ROW
    width = own.shape[2]
    wide = 2 * HEAD_DIM
    quarters = own.shape[0] * steps // 2
    here = step < steps // 2
    values = jnp.where(here, own[:, :ROW], far[:, :ROW]).reshape(rows, width).astype(F32)
    cots = jnp.where(here, own[:, ROW : 2 * ROW], far[:, ROW : 2 * ROW]).reshape(rows, width)
    grads[...] = cots
    centered = values - jnp.mean(values, axis=-1, keepdims=True)
    variance = jnp.mean(centered * centered, axis=-1, keepdims=True)
    normal = centered * lax.rsqrt(variance + EPS)
    scaled[...] = normal
    first_in = (normal * table[0:1, :] + table[1:2, :]).astype(BF)
    first[...] = first_in
    second[...] = (normal * table[2:3, :] + table[3:4, :]).astype(BF)
    joined = jnp.dot(first_in, w_joined[...], preferred_element_type=F32) + bias[...]
    grad_mixed = lax.dot_general(
        cots, w_out[...], (((1,), (1,)), ((), ())), preferred_element_type=F32
    )
    lane = lax.broadcasted_iota(jnp.int32, (rows, wide), 1)
    half = ROTARY // 2
    for block in range(4):
        piece = joined[:, block * wide : (block + 1) * wide]
        turned = jnp.where(
            lane < half, -pltpu.roll(piece, wide - half, 1), pltpu.roll(piece, half, 1)
        )
        piece = piece * cosine[...] + turned * sine[...]
        head = block % 2
        if block >= 2:
            piece = jnp.where(lane < HEAD_DIM, piece, grad_mixed[:, head * wide : (head + 1) * wide])
        piece = piece.astype(BF)
        for i in range(2):
            place = step * 2 + i
            part = piece[i * ROW : (i + 1) * ROW]
            if block < 2:
                for quarter in range(quarters):
                    msg[quarter * 2 + head, place] = part
            else:
                later = jnp.where(here, 0, 1)
                plane = place - later * quarters
                chunk = jnp.where(later == which[1], plane, quarters - 1 - plane)
                msg[chunk * 2 + head, 2 * quarters + later] = part


def front(which, own, far, table, bias, cosine, sine, w_joined, w_out):
    planes, payload_rows, width = own.shape
    steps = planes
    rows = 2 * ROW
    tokens = 2 * planes * ROW
    wide = 2 * HEAD_DIM

    def whole(array):
        return pl.BlockSpec(array.shape, lambda s: (0,) * array.ndim)

    def rowed(columns):
        return pl.BlockSpec((rows, columns), lambda s: (s, 0))

    msg_shape = (2 * planes, 2 * planes + 2, ROW, wide)
    return pl.pallas_call(
        front_kernel,
        grid=(steps,),
        out_shape=(
            jax.ShapeDtypeStruct(msg_shape, BF),
            jax.ShapeDtypeStruct((tokens, width), BF),
            jax.ShapeDtypeStruct((tokens, width), BF),
            jax.ShapeDtypeStruct((tokens, width), F32),
            jax.ShapeDtypeStruct((tokens, width), BF),
        ),
        in_specs=[
            pl.BlockSpec(memory_space=pltpu.SMEM),
            pl.BlockSpec((2, payload_rows, width), lambda s: (jnp.minimum(s, steps // 2 - 1), 0, 0)),
            pl.BlockSpec((2, payload_rows, width), lambda s: (jnp.maximum(s - steps // 2, 0), 0, 0)),
            whole(table),
            whole(bias),
            rowed(wide),
            rowed(wide),
            whole(w_joined),
            whole(w_out),
        ],
        out_specs=(
            pl.BlockSpec(msg_shape, lambda s: (0, 0, 0, 0)),
            rowed(width),
            rowed(width),
            rowed(width),
            rowed(width),
        ),
        compiler_params=pltpu.CompilerParams(vmem_limit_bytes=48 * 1024 * 1024),
        cost_estimate=pl.CostEstimate(
            flops=2 * tokens * width * 6 * wide, bytes_accessed=24 * tokens * width, transcendentals=0
        ),
        name="front",
    )(which, own, far, table, bias, cosine, sine, w_joined, w_out)


def back_kernel(
    which,
    ans,
    table,
    cosine,
    sine,
    w_joined,
    w_out,
    first,
    scaled,
    grads,
    feed,
    second,
    block_out,
    scaled_out,
    joined_grad,
    out_grad,
    sums,
):
    step = pl.program_id(0)
    wide = 2 * HEAD_DIM
    quarters = ans.shape[0] // 2
    rows = 2 * ROW
    lane = lax.broadcasted_iota(jnp.int32, (rows, wide), 1)
    half = ROTARY // 2

    @pl.when(step == 0)
    def _():
        joined_grad[...] = jnp.zeros_like(joined_grad)
        out_grad[...] = jnp.zeros_like(out_grad)
        sums[...] = jnp.zeros_like(sums)

    def turned_back(piece):
        shifted = piece * sine[...]
        shifted = jnp.where(
            lane < half,
            pltpu.roll(shifted, wide - half, 1),
            jnp.where(lane < ROTARY, -pltpu.roll(shifted, half, 1), 0.0),
        )
        return piece * cosine[...] + shifted

    key_value, mixed, query = [], [], []
    for head in range(2):
        pair, other = [], []
        for i in range(2):
            place = step * 2 + i
            total = ans[head, place].astype(F32)
            for quarter in range(1, quarters):
                total = total + ans[quarter * 2 + head, place].astype(F32)
            pair.append(total)
            later = place // quarters
            plane = place - later * quarters
            chunk = jnp.where(later == which[1], plane, quarters - 1 - plane)
            other.append(ans[chunk * 2 + head, 2 * quarters + later])
        total = jnp.concatenate(pair, axis=0).astype(BF).astype(F32)
        key_value.append(turned_back(total).astype(BF))
        other = jnp.concatenate(other, axis=0)
        mixed.append(other)
        turned = turned_back(other.astype(F32))
        query.append(jnp.where(lane < HEAD_DIM, turned, 0.0).astype(BF))
    joined = jnp.concatenate(key_value + query, axis=1)
    mixed = jnp.concatenate(mixed, axis=1)
    cots = grads[...]
    attention = jnp.dot(mixed, w_out[...], preferred_element_type=F32)
    block_out[...] = (feed[...] + attention).astype(BF)
    grad_first = lax.dot_general(
        joined, w_joined[...], (((1,), (1,)), ((), ())), preferred_element_type=F32
    )
    grad_second = second[...]
    normal = scaled[...]
    scaled_out[...] = (grad_first * table[0:1, :] + grad_second * table[2:3, :]).astype(BF)
    over_tokens = (((0,), (0,)), ((), ()))
    joined_grad[...] += lax.dot_general(
        first[...], joined, over_tokens, preferred_element_type=F32
    )
    out_grad[...] += lax.dot_general(mixed, cots, over_tokens, preferred_element_type=F32)
    sums[0:1, :] += jnp.sum(grad_first * normal, axis=0, keepdims=True)
    sums[1:2, :] += jnp.sum(grad_first, axis=0, keepdims=True)
    sums[2:3, :] += jnp.sum(grad_second * normal, axis=0, keepdims=True)
    sums[3:4, :] += jnp.sum(grad_second, axis=0, keepdims=True)
    sums[4:5, : 4 * wide] += jnp.sum(joined.astype(F32), axis=0, keepdims=True)


def back(which, ans, table, cosine, sine, w_joined, w_out, first, scaled, grads, feed, second):
    tokens, width = scaled.shape
    rows = 2 * ROW
    wide = 2 * HEAD_DIM

    def whole(shape):
        return pl.BlockSpec(shape, lambda s: (0,) * len(shape))

    def rowed(columns):
        return pl.BlockSpec((rows, columns), lambda s: (s, 0))

    return pl.pallas_call(
        back_kernel,
        grid=(tokens // rows,),
        out_shape=(
            jax.ShapeDtypeStruct((tokens, width), BF),
            jax.ShapeDtypeStruct((tokens, width), BF),
            jax.ShapeDtypeStruct(w_joined.shape, F32),
            jax.ShapeDtypeStruct(w_out.shape, F32),
            jax.ShapeDtypeStruct((8, width), F32),
        ),
        in_specs=[pl.BlockSpec(memory_space=pltpu.SMEM), whole(ans.shape), whole(table.shape)]
        + [rowed(wide)] * 2
        + [whole(w_joined.shape), whole(w_out.shape)]
        + [rowed(width)] * 5,
        out_specs=(
            rowed(width),
            rowed(width),
            whole(w_joined.shape),
            whole(w_out.shape),
            whole((8, width)),
        ),
        compiler_params=pltpu.CompilerParams(vmem_limit_bytes=48 * 1024 * 1024),
        cost_estimate=pl.CostEstimate(
            flops=2 * tokens * width * 12 * wide, bytes_accessed=24 * tokens * width, transcendentals=0
        ),
        name="back",
    )(which, ans, table, cosine, sine, w_joined, w_out, first, scaled, grads, feed, second)


def settle_kernel(which, mine, other, joined, up, down, out, vectors):
    shard_rows, wide = joined.shape[0], 2 * HEAD_DIM
    planes = up.shape[1] // 1024
    up_cols = up.shape[1] // (2 * planes)
    width = joined.shape[1] // 3
    lane = lax.broadcasted_iota(jnp.int32, (shard_rows, wide), 1) < HEAD_DIM
    total = jnp.zeros((shard_rows, wide), F32)
    first = which[1] == 0
    pair = (
        jnp.where(first, mine[...], other[...]),
        jnp.where(first, other[...], mine[...]),
    )
    side = planes // 2 * shard_rows
    for core in range(2):
        source = pair[core]
        for plane in range(planes):
            top = plane % 2 * shard_rows
            left = plane // 2 * up_cols
            blocks = [
                source[top : top + shard_rows, left + i * wide : left + (i + 1) * wide]
                for i in range(4)
            ]
            at = (2 * plane + core) * wide
            swapped = [pltpu.roll(block, HEAD_DIM, 1) for block in blocks]
            joined[:, at : at + wide] = jnp.where(lane, blocks[2], swapped[3])
            joined[:, width + at : width + at + wide] = jnp.where(lane, blocks[0], swapped[1])
            joined[:, 2 * width + at : 2 * width + at + wide] = jnp.where(
                lane, swapped[0], blocks[1]
            )
            total = total + blocks[2]
            at = (2 * plane + core) * up_cols
            up[:, at : at + up_cols] = source[
                side + top : side + top + shard_rows, left : left + up_cols
            ]
        half = down.shape[0] // 2
        down[core * half : (core + 1) * half, :] = source[2 * side : 2 * side + half]
        start = 2 * side + half
        half = out.shape[0] // 2
        out[core * half : (core + 1) * half, :] = source[start : start + half]
    vectors[...] = pltpu.roll(total, HEAD_DIM, 1)


def settle(which, mine, other, shapes):
    vmem = pl.BlockSpec(memory_space=pltpu.VMEM)
    return pl.pallas_call(
        settle_kernel,
        out_shape=tuple(jax.ShapeDtypeStruct(shape, F32) for shape in shapes),
        in_specs=[pl.BlockSpec(memory_space=pltpu.SMEM), vmem, vmem],
        out_specs=(vmem,) * len(shapes),
        compiler_params=pltpu.CompilerParams(vmem_limit_bytes=24 * 1024 * 1024),
        name="settle",
    )(which, mine, other)


def exchange(values, names):
    return lax.all_to_all(values, names, split_axis=0, concat_axis=0, tiled=True)


def core_swap(values):
    return lax.ppermute(values, "c", [(0, 1), (1, 0)])


def ring_shifts(size):
    return (1, size - 1, *range(2, size - 1))


def ring_move(values, names, size, shift):
    return lax.ppermute(values, names, [(i, (i + shift) % size) for i in range(size)])


def pin(*values):
    return lax.optimization_barrier(values)


def in_order(core, own, other):
    return jnp.where(core == 0, own, other), jnp.where(core == 0, other, own)


def normalize(values):
    mean = jnp.mean(values, axis=-1, keepdims=True)
    centered = values - mean
    inverse = lax.rsqrt(jnp.mean(centered * centered, axis=-1, keepdims=True) + EPS)
    return centered * inverse, inverse


def rotary_constants():
    half = ROTARY // 2
    wide = 2 * HEAD_DIM
    turn = np.zeros((wide, wide), np.float32)
    spread = np.zeros((half, wide), np.float32)
    keep = np.ones((wide,), np.float32)
    for i in range(half):
        turn[half + i, i] = -1.0
        turn[i, half + i] = 1.0
        spread[i, i] = 1.0
        spread[i, half + i] = 1.0
    keep[:ROTARY] = 0.0
    return turn, spread, keep


def per_device(
    hidden_in,
    positions,
    first_gain,
    first_shift,
    second_gain,
    second_shift,
    joined_weight,
    joined_bias,
    output_weight,
    output_bias,
    up_weight,
    up_bias,
    down_weight,
    down_bias,
    cotangent,
):
    rows, width = hidden_in.shape
    shard_rows = joined_weight.shape[0]
    hidden_width = up_weight.shape[1]
    wide_rows = down_weight.shape[0]
    planes = lax.axis_size("y")
    quarters = lax.axis_size("x")
    peers = quarters * lax.axis_size("zl")
    core = lax.axis_index("c")
    plane = lax.axis_index("y")
    tokens = 2 * planes * rows
    up_cols = hidden_width // (2 * planes)
    head_cols = width // (2 * planes)
    slice_index = 2 * plane + core

    whole = positions // 128
    pos_rows = jnp.stack([whole, positions - whole * 128]).astype(BF)
    pos_rows = jnp.pad(pos_rows, ((0, 14), (0, width - rows)))
    payload = jnp.concatenate([hidden_in, cotangent, pos_rows], axis=0)
    payload = exchange(jnp.broadcast_to(payload[None], (planes,) + payload.shape), "y")

    def pair_up(left, right):
        return jnp.concatenate([left, right], axis=-1)

    wj = lax.dynamic_index_in_dim(
        joined_weight.reshape(shard_rows, 3, planes, 2, 2, HEAD_DIM), core, 3, keepdims=False
    )
    vectors = jnp.concatenate(
        [
            jnp.stack(
                [first_gain, first_shift, second_gain, second_shift, output_bias, down_bias], axis=1
            ),
            joined_bias,
            up_bias.reshape(shard_rows, -1),
        ],
        axis=1,
    )
    vectors = jnp.pad(vectors, ((0, 0), (0, HEAD_DIM - vectors.shape[1])))
    vectors = jnp.broadcast_to(vectors[:, None, None], (shard_rows, planes, 2, HEAD_DIM))
    columns = jnp.concatenate([pair_up(wj[:, 1], wj[:, 2]), pair_up(wj[:, 0], vectors)], axis=2)
    columns = jnp.transpose(columns, (1, 0, 2, 3)).reshape(planes, shard_rows, -1)
    wu = lax.dynamic_index_in_dim(
        up_weight.reshape(shard_rows, planes, 2, up_cols), core, 2, keepdims=False
    )
    columns = jnp.concatenate([columns, jnp.transpose(wu, (1, 0, 2))], axis=2)
    half_out, half_down = shard_rows // 2, wide_rows // 2

    def spread_columns(columns):
        message = jnp.broadcast_to(columns[:, None], (planes, peers) + columns.shape[1:])
        message = exchange(message.reshape((planes * peers,) + columns.shape[1:]), SHARD)
        return message.reshape(width, -1)

    rows_half = jnp.concatenate(
        [
            lax.dynamic_slice_in_dim(output_weight, core * half_out, half_out, 0),
            lax.dynamic_slice_in_dim(down_weight, core * half_down, half_down, 0),
        ],
        axis=0,
    )
    rows_half = lax.all_gather(rows_half, PLANE, axis=0, tiled=False)
    payload, columns = pin(payload, columns)
    columns = spread_columns(columns)
    w_joined = columns[:, : 4 * head_cols]
    w_up = columns[:, 4 * head_cols :]
    side = 2 * head_cols + HEAD_DIM
    table = jnp.transpose(w_joined[:, side : side + 16].astype(F32))

    payload_far = core_swap(payload)
    pos = jnp.concatenate(
        [payload[:, 2 * rows : 2 * rows + 2, :rows], payload_far[:, 2 * rows : 2 * rows + 2, :rows]]
    ).astype(F32)
    pos = (pos[:, 0] * 128.0 + pos[:, 1]).reshape(1, tokens)
    turn, spread, keep = rotary_constants()
    inv_freq = 1.0 / 10000.0 ** (jnp.arange(0, ROTARY, 2, dtype=F32) / ROTARY)
    angles = pos * inv_freq[:, None]

    def to_lanes(values):
        return lax.dot_general(values, spread, (((0,), (0,)), ((), ())), precision=HIGH)

    cosine, sine = to_lanes(jnp.cos(angles)) + keep, to_lanes(jnp.sin(angles))

    own = lax.dynamic_slice_in_dim(rows_half, core * (peers // 2), peers // 2, 0)
    far = lax.dynamic_slice_in_dim(rows_half, (1 - core) * (peers // 2), peers // 2, 0)
    halves = jnp.stack(in_order(core, own, core_swap(far)), axis=1)
    w_down = halves[:, :, half_out:].reshape(up_cols, width)
    w_out = halves[:, :, :half_out].reshape(2, HEAD_DIM, width)
    w_out = jnp.pad(w_out, ((0, 0), (HEAD_DIM, 0), (0, 0))).reshape(2 * head_cols, width)

    gain_one, gain_two = table[0], table[2]
    bias_joined = lax.dynamic_slice_in_dim(table[6:9], slice_index * head_cols, head_cols, 1)
    bias_joined = bias_joined.reshape(3, 2, HEAD_DIM)
    bias_joined = jnp.concatenate(
        [
            pair_up(bias_joined[1], bias_joined[2]),
            pair_up(bias_joined[0], jnp.zeros_like(bias_joined[0])),
        ],
        axis=0,
    ).reshape(1, -1)
    bias_up = lax.dynamic_slice_in_dim(
        jnp.transpose(table[9:13]).reshape(-1), slice_index * up_cols, up_cols, 0
    )
    which = jnp.stack([lax.axis_index("x"), core]).astype(jnp.int32)
    message, first_in, second_in, scaled, grads = front(
        which, payload, payload_far, table, bias_joined, cosine, sine, w_joined, w_out
    )

    arrived = exchange(message, PLANE)

    up_pre = jnp.dot(second_in, w_up, preferred_element_type=F32) + bias_up
    activated, gelu_pull = jax.vjp(lambda v: jax.nn.gelu(v, approximate=False), up_pre)
    activated = activated.astype(BF)
    feed = jnp.dot(activated, w_down, preferred_element_type=F32)
    grad_hidden = jnp.einsum("td,fd->tf", grads, w_down, preferred_element_type=F32)
    grad_up = gelu_pull(grad_hidden)[0].astype(BF)
    grad_second = jnp.einsum("tc,fc->tf", grad_up, w_up, preferred_element_type=F32)
    up_grad = jnp.einsum("tf,tc->fc", second_in, grad_up, preferred_element_type=F32)
    down_grad = jnp.einsum("tf,td->fd", activated, grads, preferred_element_type=F32)

    def send_columns(columns):
        return exchange(columns.reshape(planes * peers, shard_rows, -1), SHARD)

    def collect_columns(columns):
        return jnp.sum(columns.reshape(planes, peers, shard_rows, -1).astype(F32), axis=1)

    def split_rows(grad, half):
        halves = grad.astype(BF).reshape(peers // 2, 2, half, width)
        own = lax.dynamic_index_in_dim(halves, core, 1, keepdims=False)
        far = core_swap(lax.dynamic_index_in_dim(halves, 1 - core, 1, keepdims=False))
        return jnp.concatenate(in_order(core, own, far), axis=0)

    arrived, up_grad, down_rows, feed, grad_second = pin(
        arrived, up_grad.astype(BF), split_rows(down_grad, half_down), feed, grad_second
    )
    up_arrived = send_columns(up_grad)
    down_sum = lax.psum_scatter(down_rows, PLANE, scatter_dimension=0, tiled=False)
    attended, up_arrived = pin(attend(arrived, which), up_arrived)
    answered = exchange(attended, PLANE)

    block_sum, grad_scaled, joined_grad, out_grad, sums = back(
        which,
        answered,
        table,
        cosine,
        sine,
        w_joined,
        w_out,
        first_in,
        scaled,
        grads,
        feed,
        grad_second,
    )
    out_grad = out_grad.reshape(2, 2, HEAD_DIM, width)[:, 1].reshape(head_cols, width)
    out_arrived = exchange(split_rows(out_grad, half_out), PLANE)

    def other_core(total):
        total = total.reshape(2, planes, rows, width)
        own, far = total[0], core_swap(total[1])
        return (own.astype(F32) + far.astype(F32)).astype(BF)

    block_sum = other_core(block_sum)
    block_moved = [
        ring_move(
            lax.dynamic_index_in_dim(block_sum, lax.rem(plane + shift, planes), 0, keepdims=False),
            "y",
            planes,
            shift,
        )
        for shift in ring_shifts(planes)
    ]
    block_sum = lax.dynamic_index_in_dim(block_sum, plane, 0, keepdims=False).astype(F32)
    grad_scaled = other_core(grad_scaled)
    totals = jnp.concatenate([sums[:4], jnp.sum(cotangent.astype(F32), axis=0)[None]], axis=0)
    joined_sum = sums[4, : 4 * head_cols].reshape(2, 2, 2, HEAD_DIM)
    joined_sum = jnp.stack([joined_sum[1, :, 0], joined_sum[0, :, 0], joined_sum[0, :, 1]])
    bias_sums = jnp.concatenate(
        [
            jnp.transpose(joined_sum.reshape(3, head_cols)),
            jnp.sum(grad_up.astype(F32), axis=0).reshape(head_cols, -1),
        ],
        axis=1,
    )
    bias_sums = lax.dynamic_update_slice_in_dim(
        jnp.zeros((width, bias_sums.shape[1]), F32), bias_sums, slice_index * head_cols, 0
    )
    vectors = jnp.concatenate([jnp.transpose(totals), bias_sums], axis=1)
    n_vectors = vectors.shape[1]
    columns = joined_grad + jnp.pad(
        vectors, ((0, 0), (side, joined_grad.shape[1] - side - n_vectors))
    )
    columns, out_arrived = pin(columns.astype(BF), out_arrived)
    columns = send_columns(columns)
    grad_scaled, columns, down_sum, *block_moved = pin(
        grad_scaled, columns, down_sum, *block_moved
    )
    grad_scaled = exchange(grad_scaled, "y")

    def beside(part):
        part = part.reshape(2, -1, up_cols)
        return jnp.concatenate([part[0], part[1]], axis=1)

    parts = [
        beside(collect_columns(columns)),
        beside(collect_columns(up_arrived)),
        down_sum.astype(F32),
        jnp.sum(out_arrived.astype(F32), axis=0),
    ]
    part = lax.reduce_precision(jnp.concatenate(parts, axis=0), 8, 7)
    far = lax.ppermute(part.astype(BF), "zh", [(0, 1), (1, 0)])
    far, grad_scaled = pin(far, grad_scaled)
    part = part + far.astype(F32)
    joined_weight_grad, up_weight_grad, down_weight_grad, output_weight_grad, vectors = settle(
        which,
        part,
        core_swap(part),
        (
            joined_weight.shape,
            up_weight.shape,
            down_weight.shape,
            output_weight.shape,
            (shard_rows, 2 * HEAD_DIM),
        ),
    )
    grad_scaled = jnp.sum(grad_scaled.astype(F32), axis=0)

    for block in block_moved:
        block_sum = block_sum + block.astype(F32)
    inputs = hidden_in.astype(F32)
    block_out = (inputs + block_sum + (table[4] + table[5])).astype(BF)
    own_scaled, inverse = normalize(inputs)
    mean_plain = jnp.mean(grad_scaled, axis=-1, keepdims=True)
    mean_scaled = jnp.mean(grad_scaled * own_scaled, axis=-1, keepdims=True)
    input_grad = (
        cotangent.astype(F32) + inverse * (grad_scaled - mean_plain - own_scaled * mean_scaled)
    ).astype(BF)
    return (
        block_out,
        input_grad,
        vectors[:, 0],
        vectors[:, 1],
        vectors[:, 2],
        vectors[:, 3],
        joined_weight_grad,
        vectors[:, 5:8],
        output_weight_grad,
        vectors[:, 4],
        up_weight_grad,
        vectors[:, 8:12].reshape(wide_rows),
        down_weight_grad,
        vectors[:, 4],
    )


def solution(mesh):
    fine = Mesh(mesh.devices.reshape(2, 2, 4, 4, 2), AXES)
    token = P(AXES, None)
    vector = P(SHARD)
    matrix = P(SHARD, None)
    in_specs = (
        (token, P(AXES))
        + (vector,) * 4
        + (matrix, matrix, matrix, vector, matrix, vector, matrix, vector, token)
    )
    out_specs = (
        (token, token)
        + (vector,) * 4
        + (matrix, matrix, matrix, vector, matrix, vector, matrix, vector)
    )
    return jax.shard_map(
        per_device, mesh=fine, in_specs=in_specs, out_specs=out_specs, check_vma=False
    )
```

time: 2390 us -> 371 us (0.16)
  waiting for transfers between devices: 1350 us -> 132 us
  blocking collectives: 599 us -> 0 us
  matrix products: 279 us -> 21.5 us
  Pallas kernels: 0 us -> 82.1 us
  local copies, waits for them, and re-layouts: 71.7 us -> 28.5 us
  starting transfers between devices: 22 us -> 61.2 us
    all_gather x8 -> x1, waiting for transfers between devices: 1000 us -> 27.8 us  [per_device(): rows_half = lax.all_gather(rows_half, PLANE, axis=0, tiled=False)]
    reduce_scatter x2 -> x1, waiting for transfers between devices: 340 us -> 0.01 us  [per_device(): lax.psum_scatter(down_rows, PLANE, scatter_dimension=0, tiled=False)]
    all_gather x4 -> x0, blocking collectives: 279 us -> none  [the longest x1 74.6 us: per_device(): lax.all_gather(log_t, 'shard', axis=1, tiled=True)]
    dot_general x52 -> x8, matrix products: 279 us -> 21.5 us  [the longest x1 6 us: per_device(): jnp.einsum('td,fd->tf', grads, w_down, preferred_element_type=F32)]
    unnamed x1 -> x0, blocking collectives: 136 us -> none
    all_to_all x2 -> x0, blocking collectives: 116 us -> none  [the longest x1 76.8 us: per_device(): lax.all_to_all(stacked, 'seq', split_axis=3, concat_axis=0, tiled=True)]
    pallas_call x0 -> x4, Pallas kernels: none -> 82.1 us  [the longest x1 59.4 us: attend(): pl.pallas_call(attention_kernel, out_shape=jax.ShapeDtypeStruct(message.s...]
    all_to_all x2 -> x8, waiting for transfers between devices: 4.45 us -> 78.5 us  [exchange(): lax.all_to_all(values, names, split_axis=0, concat_axis=0, tiled=True)]
  transfers between devices with their start and end apart: 13 -> 21, of which waited for: 8 -> 11; matrix products, arithmetic and copies ran while one was open for 15% -> 16% of each run, Pallas kernels for 0% -> 19%
where the time goes in v1:
time: 371 us; the launch traced here: 370 us
  waiting for transfers between devices  132 us (36%)
  Pallas kernels  82.1 us (22%)
  starting transfers between devices  61.2 us (16%)
  other arithmetic  29.1 us (8%)
  local copies, waits for them, and re-layouts  28.5 us (8%)
  matrix products  21.5 us (6%)
  between operations  14.8 us (4%)
    all_to_all x8, waiting for transfers between devices, exchange(): lax.all_to_all(values, names, split_axis=0, concat_axis=0, tiled=True)  78.5 us
    pallas_call x1, Pallas kernels, attend(): pl.pallas_call(attention_kernel, out_shape=jax.ShapeDtypeStruct(message.s...  59.4 us
    all_to_all x8, starting transfers between devices, exchange(): lax.all_to_all(values, names, split_axis=0, concat_axis=0, tiled=True)  45.2 us
    all_gather x1, waiting for transfers between devices, per_device(): rows_half = lax.all_gather(rows_half, PLANE, axis=0, tiled=False)  27.8 us
    ppermute x3, waiting for transfers between devices, ring_move(): lax.ppermute(values, names, [(i, (i + shift) % size) for i in range(size)])  15.8 us
    pallas_call x1, Pallas kernels, back(): pl.pallas_call(back_kernel, grid=(tokens // rows,), out_shape=(jax.ShapeD...  11.7 us
    pallas_call x1, Pallas kernels, front(): pl.pallas_call(front_kernel, grid=(steps,), out_shape=(jax.ShapeDtypeStru...  9.19 us
    ppermute x1, waiting for transfers between devices, per_device(): far = lax.ppermute(part.astype(BF), 'zh', [(0, 1), (1, 0)])  8.85 us
  transfers between devices with their start and end apart: 21, of which 11 were waited for; matrix products, arithmetic and copies ran while one was open for 16% of the time, Pallas kernels for 19%

profile of v1, /device:TPU:1, one launch (start us, length us, event | category | flops | bytes accessed | tf_op | source)
XLA Modules:
  0.0 369.5 jit_solution(6968458682020003203)
XLA Ops:
  11.4 5.2 %all-to-all-start = ((bf16[4,272,1024]{2,1,0:T(8,128)(2,1)}), bf16[4,272,1024]{2,1,0:T(8,128)(2,1)}, u32[]{:S(2)}, u32[]{:S(2)}) async-start(bf16[4,272,1024]{2,1,0:T(8,128)(2,1)} %broadcast_in_dim.10), calls=%async_computation | async-start | bytes 4456448 | tf_op jit(solution)/shard_map/all_to_all | solution.py:449
  19.6 24.4 %all-to-all-done.own = bf16[4,272,1024]{2,1,0:T(8,128)(2,1)} async-done(((bf16[4,272,1024]{2,1,0:T(8,128)(2,1)}), bf16[4,272,1024]{2,1,0:T(8,128)(2,1)}, u32[]{:S(2)}, u32[]{:S(2)}) %all-to-all-start) | async-done | bytes 2228256 | tf_op jit(solution)/shard_map/all_to_all | solution.py:449
  45.6 6.5 %all-to-all-start.1 = ((bf16[32,32,1024]{2,1,0:T(8,128)(2,1)}), bf16[32,32,1024]{2,1,0:T(8,128)(2,1)S(1)}, u32[]{:S(2)}, u32[]{:S(2)}) async-start(bf16[32,32,1024]{2,1,0:T(8,128)(2,1)} %bitcast.17), calls=%async_computation.1 | async-start | bytes 4194304 | tf_op jit(solution)/shard_map/all_to_all | solution.py:449
  54.0 27.8 %all-gather.3.cloned.1.call-done = bf16[640,1024]{1,0:T(8,128)(2,1)} async-done(((bf16[80,1024]{1,0:T(8,128)(2,1)}), bf16[640,1024]{1,0:T(8,128)(2,1)}) %all-gather.3.cloned.1.call-update) | async-done | bytes 1310736 | tf_op jit(solution)/shard_map/all_gather | solution.py:569
  98.5 9.2 %front.1 = (bf16[8,10,128,128]{3,2,1,0:T(8,128)(2,1)}, bf16[1024,1024]{1,0:T(8,128)(2,1)S(1)}, bf16[1024,1024]{1,0:T(8,128)(2,1)}, f32[1024,1024]{1,0:T(8,128)}, bf16[1024,1024]{1,0:T(8,128)(2,1)}) custom-call(s32[2]{0:T(128)S(1)} %pad_add_fusion.which, bf16[4,272,1024]{2,1,0:T(8,128)(2,1)} %all-to-all-done.own, ...), custom_call_target="tpu_custom_call" | custom-call | flops 1610612736 | bytes 25165824 | tf_op jit(solution)/shard_map/front/pallas_call | solution.py:235
  109.1 6.7 %all-to-all-start.2 = ((bf16[8,10,128,128]{3,2,1,0:T(8,128)(2,1)}), bf16[8,10,128,128]{3,2,1,0:T(8,128)(2,1)}, u32[]{:S(2)}, u32[]{:S(2)}) async-start(bf16[8,10,128,128]{3,2,1,0:T(8,128)(2,1)} %get-tuple-element.50), calls=%async_computation.2 | async-start | bytes 5242880 | tf_op jit(solution)/shard_map/all_to_all | solution.py:449
  115.8 3.2 fusion.10
  119.1 6.0 %convert_reduce_fusion.4 = (f32[512]{0:T(512)S(1)}, bf16[1024,512]{1,0:T(8,128)(2,1)S(1)}, f32[1024,512]{1,0:T(8,128)S(1)}) fusion(f32[1024,512]{1,0:T(8,128)S(1)} %fusion.10, f32[512]{0:T(512)S(1)} %dynamic_slice.60, bf16[1024,1024]{1,0:T(8,128)(2,1)S(1)} %copy-done.7, bf16[512,1024]{1,0:T(8,128)(2,1)S(1)} %bitcast.143), kind=kOutput, calls=%fused_computation.11 | convolution fusion | flops 1113062912 | bytes 8392704 | tf_op jit(solution)/shard_map/td,fd->tf/dot_general | solution.py:622
  127.7 3.2 fusion.44.feed
  131.0 2.3 convolution_convert_fusion.1
  133.3 3.3 fusion.8.second
  137.8 16.1 %all-to-all-done.2.msg = bf16[8,10,128,128]{3,2,1,0:T(8,128)(2,1)} async-done(((bf16[8,10,128,128]{3,2,1,0:T(8,128)(2,1)}), bf16[8,10,128,128]{3,2,1,0:T(8,128)(2,1)}, u32[]{:S(2)}, u32[]{:S(2)}) %all-to-all-start.2) | async-done | bytes 2621472 | tf_op jit(solution)/shard_map/all_to_all | solution.py:449
  153.9 6.1 %all-to-all-start.3 = ((bf16[32,32,512]{2,1,0:T(8,128)(2,1)}), bf16[32,32,512]{2,1,0:T(8,128)(2,1)}, u32[]{:S(2)}, u32[]{:S(2)}) async-start(bf16[32,32,512]{2,1,0:T(8,128)(2,1)} %bitcast.145), calls=%async_computation.3 | async-start | bytes 2097152 | tf_op jit(solution)/shard_map/all_to_all | solution.py:449
  159.9 59.4 %attention.1 = bf16[8,10,128,128]{3,2,1,0:T(8,128)(2,1)S(1)} custom-call(s32[2]{0:T(128)S(1)} %pad_add_fusion.which, bf16[8,10,128,128]{3,2,1,0:T(8,128)(2,1)} %all-to-all-done.2.msg), custom_call_target="tpu_custom_call" | custom-call | flops 8455716864 | bytes 5242880 | tf_op jit(solution)/shard_map/attention/pallas_call | solution.py:146
  220.8 4.9 %all-to-all-start.4 = ((bf16[8,10,128,128]{3,2,1,0:T(8,128)(2,1)}), bf16[8,10,128,128]{3,2,1,0:T(8,128)(2,1)}, u32[]{:S(2)}, u32[]{:S(2)}) async-start(bf16[8,10,128,128]{3,2,1,0:T(8,128)(2,1)} %copy-done.2), calls=%async_computation.4 | async-start | bytes 5242880 | tf_op jit(solution)/shard_map/all_to_all | solution.py:449
  228.2 2.1 convert_reduce_fusion.2
  230.3 31.7 %all-to-all-done.4.ans = bf16[8,10,128,128]{3,2,1,0:T(8,128)(2,1)} async-done(((bf16[8,10,128,128]{3,2,1,0:T(8,128)(2,1)}), bf16[8,10,128,128]{3,2,1,0:T(8,128)(2,1)}, u32[]{:S(2)}, u32[]{:S(2)}) %all-to-all-start.4) | async-done | bytes 2621472 | tf_op jit(solution)/shard_map/all_to_all | solution.py:449
  262.1 11.7 %back.1 = (bf16[1024,1024]{1,0:T(8,128)(2,1)S(1)}, bf16[1024,1024]{1,0:T(8,128)(2,1)}, f32[1024,512]{1,0:T(8,128)}, f32[256,1024]{1,0:T(8,128)S(1)}, f32[8,1024]{1,0:T(8,128)S(1)}) custom-call(s32[2]{0:T(128)S(1)} %pad_add_fusion.which, bf16[8,10,128,128]{3,2,1,0:T(8,128)(2,1)} %all-to-all-done.4.ans, f32[16,1024]{1,0:T(8,128)S(1)} %copy.107.table, ...), custom_call_target="tpu_custom_call" | custom-call | flops 3221225472 | bytes 25165824 | tf_op jit(solution)/shard_map/back/pallas_call | solution.py:365
  278.7 2.4 collective-permute-start.5
  281.1 3.7 %fusion.39 = (bf16[512,1024]{1,0:T(8,128)(2,1)}, bf16[512,1024]{1,0:T(8,128)(2,1)}, bf16[512,1024]{1,0:T(8,128)(2,1)}, bf16[512,1024]{1,0:T(8,128)(2,1)}) fusion(bf16[1024,1024]{1,0:T(8,128)(2,1)S(1)} %copy-done.5, bf16[1024,1024]{1,0:T(8,128)(2,1)} %get-tuple-element.61), kind=kLoop, calls=%fused_computation.136 | loop fusion | bytes 8388608 | tf_op jit(solution)/shard_map/slice | solution.py:667
  287.4 4.9 %all-to-all-start.5 = ((bf16[8,16,1024]{2,1,0:T(8,128)(2,1)}), bf16[8,16,1024]{2,1,0:T(8,128)(2,1)}, u32[]{:S(2)}, u32[]{:S(2)}) async-start(bf16[8,16,1024]{2,1,0:T(8,128)(2,1)} %pad_maximum_fusion.5), calls=%async_computation.5 | async-start | bytes 524288 | tf_op jit(solution)/shard_map/all_to_all | solution.py:449
  293.8 5.4 %all-to-all-done.5 = bf16[8,16,1024]{2,1,0:T(8,128)(2,1)} async-done(((bf16[8,16,1024]{2,1,0:T(8,128)(2,1)}), bf16[8,16,1024]{2,1,0:T(8,128)(2,1)}, u32[]{:S(2)}, u32[]{:S(2)}) %all-to-all-start.5) | async-done | bytes 262176 | tf_op jit(solution)/shard_map/all_to_all | solution.py:449
  299.2 6.7 %all-to-all-start.6 = ((bf16[32,32,512]{2,1,0:T(8,128)(2,1)}), bf16[32,32,512]{2,1,0:T(8,128)(2,1)S(1)}, u32[]{:S(2)}, u32[]{:S(2)}) async-start(bf16[32,32,512]{2,1,0:T(8,128)(2,1)} %bitcast.46), calls=%async_computation.6 | async-start | bytes 2097152 | tf_op jit(solution)/shard_map/all_to_all | solution.py:449
  307.0 2.0 fusion.2
  310.0 2.7 collective-permute-start.8
  314.2 2.5 fusion.1
  316.7 9.8 %collective-permute-done.8 = bf16[128,1024]{1,0:T(8,128)(2,1)S(1)} collective-permute-done((bf16[128,1024]{1,0:T(8,128)(2,1)}, bf16[128,1024]{1,0:T(8,128)(2,1)S(1)}, u32[]{:S(2)}, u32[]{:S(2)}) %collective-permute-start.8) | collective-permute-done | bytes 262176 | tf_op jit(solution)/shard_map/ppermute | solution.py:461
  326.4 4.5 %collective-permute-done.7 = bf16[128,1024]{1,0:T(8,128)(2,1)S(1)} collective-permute-done((bf16[128,1024]{1,0:T(8,128)(2,1)}, bf16[128,1024]{1,0:T(8,128)(2,1)S(1)}, u32[]{:S(2)}, u32[]{:S(2)}) %collective-permute-start.7) | collective-permute-done | bytes 262176 | tf_op jit(solution)/shard_map/ppermute | solution.py:461
  332.5 4.3 %all-to-all-start.7 = ((bf16[4,128,1024]{2,1,0:T(8,128)(2,1)}), bf16[4,128,1024]{2,1,0:T(8,128)(2,1)}, u32[]{:S(2)}, u32[]{:S(2)}) async-start(bf16[4,128,1024]{2,1,0:T(8,128)(2,1)} %fusion.1), calls=%async_computation.8 | async-start | bytes 2097152 | tf_op jit(solution)/shard_map/all_to_all | solution.py:449
  338.0 3.1 collective-permute-start.9
  341.8 8.8 %collective-permute-done.9 = bf16[208,1024]{1,0:T(8,128)(2,1)} collective-permute-done((bf16[208,1024]{1,0:T(8,128)(2,1)S(1)}, bf16[208,1024]{1,0:T(8,128)(2,1)}, u32[]{:S(2)}, u32[]{:S(2)}) %collective-permute-start.9) | collective-permute-done | bytes 426016 | tf_op jit(solution)/shard_map/ppermute | solution.py:718
  356.0 2.1 fusion.20
  (202 shorter events, 62.1 us)
Async XLA Ops:
  7.2 9.4 %copy-start = (bf16[128,1024]{1,0:T(8,128)(2,1)S(1)}, bf16[128,1024]{1,0:T(8,128)(2,1)}, u32[]{:S(2)}) copy-start(bf16[128,1024]{1,0:T(8,128)(2,1)} %param.29) | copy-start | bytes 786436
  11.4 6.4 %copy-start.25 = (bf16[32,3]{0,1:T(4,128)(2,1)S(1)}, bf16[32,3]{0,1:T(4,128)(2,1)}, u32[]{:S(2)}) copy-start(bf16[32,3]{0,1:T(4,128)(2,1)} %param.24) | copy-start | bytes 580
  11.4 6.5 %copy-start.31 = (bf16[32]{0:T(256)(128)(2,1)S(1)}, bf16[32]{0:T(256)(128)(2,1)}, u32[]{:S(2)}) copy-start(bf16[32]{0:T(256)(128)(2,1)} %param.26) | copy-start | bytes 196
  11.4 6.6 %copy-start.32 = (bf16[128]{0:T(256)(128)(2,1)S(1)}, bf16[128]{0:T(256)(128)(2,1)}, u32[]{:S(2)}) copy-start(bf16[128]{0:T(256)(128)(2,1)} %param.28) | copy-start | bytes 772
  11.4 6.7 %copy-start.33 = (bf16[32]{0:T(256)(128)(2,1)S(1)}, bf16[32]{0:T(256)(128)(2,1)}, u32[]{:S(2)}) copy-start(bf16[32]{0:T(256)(128)(2,1)} %param.30) | copy-start | bytes 196
  11.4 6.8 %copy-start.21 = (bf16[32,4096]{1,0:T(8,128)(2,1)S(1)}, bf16[32,4096]{1,0:T(8,128)(2,1)}, u32[]{:S(2)}) copy-start(bf16[32,4096]{1,0:T(8,128)(2,1)} %param.27) | copy-start | bytes 786436
  11.4 32.5 %all-to-all-start = ((bf16[4,272,1024]{2,1,0:T(8,128)(2,1)}), bf16[4,272,1024]{2,1,0:T(8,128)(2,1)}, u32[]{:S(2)}, u32[]{:S(2)}) async-start(bf16[4,272,1024]{2,1,0:T(8,128)(2,1)} %broadcast_in_dim.10), calls=%async_computation | async-start | bytes 4456448 | tf_op jit(solution)/shard_map/all_to_all | solution.py:449
  16.6 65.2 %all-gather.3.cloned.1.call-start = ((), (), s32[]{:S(2)}) async-start(), calls=%async_computation.10 | async-start | bytes 1474560 | tf_op jit(solution)/shard_map/all_gather | solution.py:569
  45.6 44.2 %all-to-all-start.1 = ((bf16[32,32,1024]{2,1,0:T(8,128)(2,1)}), bf16[32,32,1024]{2,1,0:T(8,128)(2,1)S(1)}, u32[]{:S(2)}, u32[]{:S(2)}) async-start(bf16[32,32,1024]{2,1,0:T(8,128)(2,1)} %bitcast.17), calls=%async_computation.1 | async-start | bytes 4194304 | tf_op jit(solution)/shard_map/all_to_all | solution.py:449
  52.0 43.5 %collective-permute-start = (bf16[4,272,1024]{2,1,0:T(8,128)(2,1)}, bf16[4,272,1024]{2,1,0:T(8,128)(2,1)}, u32[]{:S(2)}, u32[]{:S(2)}) collective-permute-start(bf16[4,272,1024]{2,1,0:T(8,128)(2,1)} %all-to-all-done.own), channel_id=1, source_target_pairs={{0,32},{32,0},{1,33},{33,1},{2,34},{34,2},{3,35},{35,3},{4,36},{36... | collective-permute-start | bytes 6684680 | tf_op jit(solution)/shard_map/ppermute | solution.py:453
  83.8 3.5 collective-permute-start.1
  109.1 44.8 %all-to-all-start.2 = ((bf16[8,10,128,128]{3,2,1,0:T(8,128)(2,1)}), bf16[8,10,128,128]{3,2,1,0:T(8,128)(2,1)}, u32[]{:S(2)}, u32[]{:S(2)}) async-start(bf16[8,10,128,128]{3,2,1,0:T(8,128)(2,1)} %get-tuple-element.50), calls=%async_computation.2 | async-start | bytes 5242880 | tf_op jit(solution)/shard_map/all_to_all | solution.py:449
  127.0 9.6 %collective-permute-start.2 = (bf16[4,64,1024]{2,1,0:T(8,128)(2,1)S(1)}, bf16[4,64,1024]{2,1,0:T(8,128)(2,1)S(1)}, u32[]{:S(2)}, u32[]{:S(2)}) collective-permute-start(bf16[4,64,1024]{2,1,0:T(8,128)(2,1)S(1)} %dynamic-slice_bitcast_fusion), channel_id=1, source_target_pairs={{0,32},{32,0},{1,33},{33,1},{2,34},{34,2},{3,35},{35,3},{4,36},{36... | collective-permute-start | bytes 1572872 | tf_op jit(solution)/shard_map/ppermute | solution.py:453
  153.9 66.9 %all-to-all-start.3 = ((bf16[32,32,512]{2,1,0:T(8,128)(2,1)}), bf16[32,32,512]{2,1,0:T(8,128)(2,1)}, u32[]{:S(2)}, u32[]{:S(2)}) async-start(bf16[32,32,512]{2,1,0:T(8,128)(2,1)} %bitcast.145), calls=%async_computation.3 | async-start | bytes 2097152 | tf_op jit(solution)/shard_map/all_to_all | solution.py:449
  220.8 41.3 %all-to-all-start.4 = ((bf16[8,10,128,128]{3,2,1,0:T(8,128)(2,1)}), bf16[8,10,128,128]{3,2,1,0:T(8,128)(2,1)}, u32[]{:S(2)}, u32[]{:S(2)}) async-start(bf16[8,10,128,128]{3,2,1,0:T(8,128)(2,1)} %copy-done.2), calls=%async_computation.4 | async-start | bytes 5242880 | tf_op jit(solution)/shard_map/all_to_all | solution.py:449
  225.6 91.1 %reduce-scatter.2.cloned.1.call-start = ((), (), s32[]{:S(2)}) async-start(), calls=%async_computation.9 | async-start | bytes 1179648 | tf_op jit(solution)/shard_map/reduce_scatter | solution.py:644
  278.7 7.1 %collective-permute-start.5 = (bf16[4,16,1024]{2,1,0:T(8,128)(2,1)S(1)}, bf16[4,16,1024]{2,1,0:T(8,128)(2,1)S(1)}, u32[]{:S(2)}, u32[]{:S(2)}) collective-permute-start(bf16[4,16,1024]{2,1,0:T(8,128)(2,1)S(1)} %dynamic-slice_bitcast_fusion.4), channel_id=1, source_target_pairs={{0,32},{32,0},{1,33},{33,1},{2,34},{34,2},{3,35},{35,3},{4,36},{36... | collective-permute-start | bytes 393224 | tf_op jit(solution)/shard_map/ppermute | solution.py:453
  284.9 7.5 %copy-start.13 = (f32[1024,512]{1,0:T(8,128)S(1)}, f32[1024,512]{1,0:T(8,128)}, u32[]{:S(2)}) copy-start(f32[1024,512]{1,0:T(8,128)} %get-tuple-element.62) | copy-start | bytes 6291460
  284.9 22.1 %collective-permute-start.3 = (bf16[4,128,1024]{2,1,0:T(8,128)(2,1)}, bf16[4,128,1024]{2,1,0:T(8,128)(2,1)}, u32[]{:S(2)}, u32[]{:S(2)}) collective-permute-start(bf16[4,128,1024]{2,1,0:T(8,128)(2,1)} %bitcast.35), channel_id=1, source_target_pairs={{0,32},{32,0},{1,33},{33,1},{2,34},{34,2},{3,35},{35,3},{4,36},{36... | collective-permute-start | bytes 3145736 | tf_op jit(solution)/shard_map/ppermute | solution.py:453
  285.2 29.0 %collective-permute-start.4 = (bf16[4,128,1024]{2,1,0:T(8,128)(2,1)}, bf16[4,128,1024]{2,1,0:T(8,128)(2,1)}, u32[]{:S(2)}, u32[]{:S(2)}) collective-permute-start(bf16[4,128,1024]{2,1,0:T(8,128)(2,1)} %bitcast.149), channel_id=1, source_target_pairs={{0,32},{32,0},{1,33},{33,1},{2,34},{34,2},{3,35},{35,3},{4,36},{36... | collective-permute-start | bytes 3145736 | tf_op jit(solution)/shard_map/ppermute | solution.py:453
  287.4 11.8 %all-to-all-start.5 = ((bf16[8,16,1024]{2,1,0:T(8,128)(2,1)}), bf16[8,16,1024]{2,1,0:T(8,128)(2,1)}, u32[]{:S(2)}, u32[]{:S(2)}) async-start(bf16[8,16,1024]{2,1,0:T(8,128)(2,1)} %pad_maximum_fusion.5), calls=%async_computation.5 | async-start | bytes 524288 | tf_op jit(solution)/shard_map/all_to_all | solution.py:449
  292.4 13.6 %copy-start.14 = (f32[4,32,512]{2,1,0:T(8,128)S(1)}, f32[4,32,512]{2,1,0:T(8,128)}, u32[]{:S(2)}) copy-start(f32[4,32,512]{2,1,0:T(8,128)} %convert_reduce_fusion.2) | copy-start | bytes 786436
  299.2 33.2 %all-to-all-start.6 = ((bf16[32,32,512]{2,1,0:T(8,128)(2,1)}), bf16[32,32,512]{2,1,0:T(8,128)(2,1)S(1)}, u32[]{:S(2)}, u32[]{:S(2)}) async-start(bf16[32,32,512]{2,1,0:T(8,128)(2,1)} %bitcast.46), calls=%async_computation.6 | async-start | bytes 2097152 | tf_op jit(solution)/shard_map/all_to_all | solution.py:449
  307.0 7.2 %copy-start.11 = (bf16[512,1024]{1,0:T(8,128)(2,1)S(1)}, bf16[512,1024]{1,0:T(8,128)(2,1)}, u32[]{:S(2)}) copy-start(bf16[512,1024]{1,0:T(8,128)(2,1)} %get-tuple-element.178) | copy-start | bytes 3145732
  310.0 16.5 %collective-permute-start.8 = (bf16[128,1024]{1,0:T(8,128)(2,1)}, bf16[128,1024]{1,0:T(8,128)(2,1)S(1)}, u32[]{:S(2)}, u32[]{:S(2)}) collective-permute-start(bf16[128,1024]{1,0:T(8,128)(2,1)} %get-tuple-element.161), channel_id=1, source_target_pairs={{0,16},{8,24},{16,0},{24,8},{1,17},{9,25},{17,1},{25,9},{2,18},{10... | collective-permute-start | bytes 786440 | tf_op jit(solution)/shard_map/ppermute | solution.py:461
  312.7 18.2 %collective-permute-start.7 = (bf16[128,1024]{1,0:T(8,128)(2,1)}, bf16[128,1024]{1,0:T(8,128)(2,1)S(1)}, u32[]{:S(2)}, u32[]{:S(2)}) collective-permute-start(bf16[128,1024]{1,0:T(8,128)(2,1)} %get-tuple-element.162), channel_id=1, source_target_pairs={{0,24},{8,0},{16,8},{24,16},{1,25},{9,1},{17,9},{25,17},{2,26},{10... | collective-permute-start | bytes 786440 | tf_op jit(solution)/shard_map/ppermute | solution.py:461
  313.6 18.9 %collective-permute-start.6 = (bf16[128,1024]{1,0:T(8,128)(2,1)}, bf16[128,1024]{1,0:T(8,128)(2,1)}, u32[]{:S(2)}, u32[]{:S(2)}) collective-permute-start(bf16[128,1024]{1,0:T(8,128)(2,1)} %get-tuple-element.163), channel_id=1, source_target_pairs={{0,8},{8,16},{16,24},{24,0},{1,9},{9,17},{17,25},{25,1},{2,10},{10... | collective-permute-start | bytes 786440 | tf_op jit(solution)/shard_map/ppermute | solution.py:461
  332.5 19.1 %all-to-all-start.7 = ((bf16[4,128,1024]{2,1,0:T(8,128)(2,1)}), bf16[4,128,1024]{2,1,0:T(8,128)(2,1)}, u32[]{:S(2)}, u32[]{:S(2)}) async-start(bf16[4,128,1024]{2,1,0:T(8,128)(2,1)} %fusion.1), calls=%async_computation.8 | async-start | bytes 2097152 | tf_op jit(solution)/shard_map/all_to_all | solution.py:449
  338.0 12.7 %collective-permute-start.9 = (bf16[208,1024]{1,0:T(8,128)(2,1)S(1)}, bf16[208,1024]{1,0:T(8,128)(2,1)}, u32[]{:S(2)}, u32[]{:S(2)}) collective-permute-start(bf16[208,1024]{1,0:T(8,128)(2,1)S(1)} %fusion.26), channel_id=1, source_target_pairs={{0,64},{64,0},{1,65},{65,1},{2,66},{66,2},{3,67},{67,3},{4,68},{68... | collective-permute-start | bytes 1277960 | tf_op jit(solution)/shard_map/ppermute | solution.py:718
  341.8 14.2 %copy-start.12 = (bf16[128,1024]{1,0:T(8,128)(2,1)S(1)}, bf16[128,1024]{1,0:T(8,128)(2,1)}, u32[]{:S(2)}) copy-start(bf16[128,1024]{1,0:T(8,128)(2,1)} %param.31) | copy-start | bytes 786436
  354.3 3.8 %collective-permute-start.10 = (f32[208,1024]{1,0:T(8,128)S(1)}, f32[208,1024]{1,0:T(8,128)S(1)}, u32[]{:S(2)}, u32[]{:S(2)}) collective-permute-start(f32[208,1024]{1,0:T(8,128)S(1)} %convert_add_fusion.2.mine), channel_id=1, source_target_pairs={{0,32},{32,0},{1,33},{33,1},{2,34},{34,2},{3,35},{35,3},{4,36},{36... | collective-permute-start | bytes 2555912 | tf_op jit(solution)/shard_map/ppermute | solution.py:453
  356.0 6.7 %copy-start.1 = (bf16[128,1024]{1,0:T(8,128)(2,1)S(1)}, bf16[128,1024]{1,0:T(8,128)(2,1)}, u32[]{:S(2)}) copy-start(bf16[128,1024]{1,0:T(8,128)(2,1)} %param.29) | copy-start | bytes 786436
  (25 other events, 91.1 us)
Sparse Core Ops, SparseCore 0:
  19.6 62.0 all-gather.2
  228.9 52.4 reduce-scatter.1

commit v2 on v1

--- a/solution.py
+++ b/solution.py
@@ -23,118 +23,158 @@
 SHARD = ("y", "x", "zl")
 
 
-def attention_kernel(which, msg, out, kv, kvt, qg, qz, gz, dkv):
+def attention_kernel(which, msg, out, kv, kvt, qg, qz, gz, dkv, held, tops):
     sources, blocks = msg.shape[0], msg.shape[1]
     chunks = blocks - 2
     span = sources * ROW
-    low_rows = lax.broadcasted_iota(jnp.int32, (2 * HEAD_DIM, ROW), 0) < HEAD_DIM
-    low_lanes = lax.broadcasted_iota(jnp.int32, (ROW, 2 * HEAD_DIM), 1) < HEAD_DIM
-
-    def key_place(source, place):
+    wide = 2 * HEAD_DIM
+    low_rows = lax.broadcasted_iota(jnp.int32, (wide, span), 0) < HEAD_DIM
+    low_lanes = lax.broadcasted_iota(jnp.int32, (ROW, wide), 1) < HEAD_DIM
+    one = (
+        lax.broadcasted_iota(jnp.int32, (wide, wide), 0)
+        == lax.broadcasted_iota(jnp.int32, (wide, wide), 1)
+    ).astype(BF)
+
+    def turned(rows):
+        return lax.dot_general(one, rows, (((1,), (1,)), ((), ())), preferred_element_type=F32)
+
+    def key_place(place):
         chunk = lax.rem(place + which[1] * (chunks // 2), chunks)
-        return pl.multiple_of(chunk * span + source * ROW, ROW)
-
-    def load_keys(index, carry):
-        source, place = index // chunks, index % chunks
-        at = key_place(source, place)
-        block = msg[source, place]
-        kv[pl.ds(at, ROW), :] = block
-        kvt[:, pl.ds(at, ROW)] = block.astype(F32).T.astype(BF)
-        dkv[pl.ds(at, ROW), :] = jnp.zeros((ROW, 2 * HEAD_DIM), F32)
+        return pl.multiple_of(chunk * span, span)
+
+    def load_keys(place, carry):
+        at = key_place(place)
+        for source in range(sources):
+            kv[pl.ds(at + source * ROW, ROW), :] = msg[source, place]
+        kvt[:, pl.ds(at, span)] = turned(kv[pl.ds(at, span), :]).astype(BF)
+        dkv[pl.ds(at, span), :] = jnp.zeros((span, wide), F32)
         return carry
 
-    lax.fori_loop(0, sources * chunks, load_keys, 0)
-
-    def load_queries(index, carry):
-        source, part = index // 2, index % 2
-        at = pl.multiple_of(part * span + source * ROW, ROW)
-        block = msg[source, chunks + part].astype(F32)
-        block = jnp.where(low_lanes, block * (HEAD_DIM**-0.5), block)
-        qg[pl.ds(at, ROW), :] = block.astype(BF)
-        turned = block.T
-        qz[:, pl.ds(at, ROW)] = jnp.where(low_rows, turned, 0.0).astype(BF)
-        gz[:, pl.ds(at, ROW)] = jnp.where(low_rows, 0.0, turned).astype(BF)
+    lax.fori_loop(0, chunks, load_keys, 0)
+
+    def load_queries(part, carry):
+        at = pl.multiple_of(part * span, span)
+        for source in range(sources):
+            block = msg[source, chunks + part].astype(F32)
+            block = jnp.where(low_lanes, block * (HEAD_DIM**-0.5), block)
+            qg[pl.ds(at + source * ROW, ROW), :] = block.astype(BF)
+        both = turned(qg[pl.ds(at, span), :])
+        qz[:, pl.ds(at, span)] = jnp.where(low_rows, both, 0.0).astype(BF)
+        gz[:, pl.ds(at, span)] = jnp.where(low_rows, 0.0, both).astype(BF)
         return carry
 
-    lax.fori_loop(0, sources * 2, load_queries, 0)
-    tiles = span // QT
+    lax.fori_loop(0, 2, load_queries, 0)
     lanes_tile = lax.broadcasted_iota(jnp.int32, (QT, 2 * HEAD_DIM), 1) < HEAD_DIM
     causal = lax.broadcasted_iota(jnp.int32, (KT, QT), 0) <= lax.broadcasted_iota(
         jnp.int32, (KT, QT), 1
     )
-
-    def one_tile(index, carry):
-        part, tile = index // tiles, index % tiles
+    tiles = span // QT
+
+    def one_part(part, carry):
         chunk = jnp.where(part == which[1], which[0], chunks - 1 - which[0])
-        at = pl.multiple_of(index * QT, QT)
-        full = chunk * (span // KT) + tile
-        query_t = qz[:, pl.ds(at, QT)]
-        grad_t = gz[:, pl.ds(at, QT)]
-
-        def forward(step, state, masked):
-            best, total, summed = state
-            k_at = pl.multiple_of(step * KT, KT)
-            scores = jnp.dot(kv[pl.ds(k_at, KT), :], query_t, preferred_element_type=F32)
-            if masked:
-                scores = jnp.where(causal, scores, NEG)
-            new_best = jnp.maximum(best, jnp.max(scores, axis=0, keepdims=True))
-            probs = jnp.exp(scores - new_best)
-            factor = jnp.exp(best - new_best)
-            total = total * factor + jnp.sum(probs, axis=0, keepdims=True)
-            summed = summed * factor + jnp.dot(
-                kvt[HEAD_DIM:, pl.ds(k_at, KT)], probs.astype(BF), preferred_element_type=F32
-            )
-            return new_best, total, summed
-
-        state = (
-            jnp.full((1, QT), NEG, F32),
-            jnp.zeros((1, QT), F32),
-            jnp.zeros((HEAD_DIM, QT), F32),
-        )
-        state = lax.fori_loop(0, full, lambda s, v: forward(s, v, False), state)
-        best, total, summed = forward(full, state, True)
-        mixed = (summed / total).astype(BF).astype(F32)
-        log_rows = best + jnp.log(total)
-        delta = jnp.sum(mixed * grad_t[HEAD_DIM:, :].astype(F32), axis=0, keepdims=True)
-        both = qg[pl.ds(at, QT), :]
-        zero = jnp.zeros_like(both)
-        only_query = jnp.where(lanes_tile, both, zero)
-        only_grad = jnp.where(lanes_tile, zero, both)
-
-        def backward(step, grad_query, masked):
+        full = chunk * tiles
+        spots = [pl.multiple_of(part * span + tile * QT, QT) for tile in range(tiles)]
+        query_t = [qz[:, pl.ds(at, QT)] for at in spots]
+        grad_t = [gz[:, pl.ds(at, QT)] for at in spots]
+
+        def forward(step, states, diagonal=None):
             k_at = pl.multiple_of(step * KT, KT)
             block = kv[pl.ds(k_at, KT), :]
-            scores = jnp.dot(block, query_t, preferred_element_type=F32)
-            probs = jnp.exp(scores - log_rows)
-            if masked:
-                probs = jnp.where(causal, probs, 0.0)
-            grad_probs = jnp.dot(block, grad_t, preferred_element_type=F32)
-            grad_scores = (probs * (grad_probs - delta)).astype(BF)
-            dkv[pl.ds(k_at, KT), :] += jnp.dot(
-                grad_scores, only_query, preferred_element_type=F32
-            ) + jnp.dot(probs.astype(BF), only_grad, preferred_element_type=F32)
-            return grad_query + jnp.dot(
-                kvt[:HEAD_DIM, pl.ds(k_at, KT)], grad_scores, preferred_element_type=F32
+            block_t = kvt[HEAD_DIM:, pl.ds(k_at, KT)]
+            start = 0 if diagonal is None else diagonal
+            scores = [
+                jnp.dot(block, query_t[tile], preferred_element_type=F32)
+                for tile in range(start, tiles)
+            ]
+            results = list(states)
+            for tile in range(start, tiles):
+                best, total, summed = states[tile]
+                score = scores[tile - start]
+                if tile == diagonal:
+                    score = jnp.where(causal, score, NEG)
+                new_best = jnp.maximum(best, jnp.max(score, axis=0, keepdims=True))
+                probs = jnp.exp(score - new_best)
+                factor = jnp.exp(best - new_best)
+                total = total * factor + jnp.sum(probs, axis=0, keepdims=True)
+                probs = probs.astype(BF)
+                held[pl.ds(k_at, KT), tile * QT : (tile + 1) * QT] = probs
+                tops[pl.ds(step, 1), tile * QT : (tile + 1) * QT] = new_best
+                summed = summed * factor + jnp.dot(block_t, probs, preferred_element_type=F32)
+                results[tile] = (new_best, total, summed)
+            return tuple(results)
+
+        states = tuple(
+            (
+                jnp.full((1, QT), NEG, F32),
+                jnp.zeros((1, QT), F32),
+                jnp.zeros((HEAD_DIM, QT), F32),
             )
-
-        grad_query = jnp.zeros((HEAD_DIM, QT), F32)
-        grad_query = lax.fori_loop(0, full, lambda s, v: backward(s, v, False), grad_query)
-        grad_query = backward(full, grad_query, True) * (HEAD_DIM**-0.5)
-        result = jnp.concatenate([grad_query, mixed], axis=0).T.astype(BF)
-        for piece in range(QT // ROW):
-            out[tile * (QT // ROW) + piece, chunks + part] = result[
-                piece * ROW : (piece + 1) * ROW
+            for _ in range(tiles)
+        )
+        states = lax.fori_loop(0, full, forward, states)
+        for tile in range(tiles):
+            states = forward(full + tile, states, tile)
+        mixed, log_rows, delta, only_query, only_grad = [], [], [], [], []
+        for tile, (best, total, summed) in enumerate(states):
+            mixed.append((summed / total).astype(BF).astype(F32))
+            log_rows.append(best + jnp.log(total))
+            delta.append(
+                jnp.sum(
+                    mixed[tile] * grad_t[tile][HEAD_DIM:, :].astype(F32), axis=0, keepdims=True
+                )
+            )
+            both = qg[pl.ds(spots[tile], QT), :]
+            zero = jnp.zeros_like(both)
+            only_query.append(jnp.where(lanes_tile, both, zero))
+            only_grad.append(jnp.where(lanes_tile, zero, both))
+
+        def backward(step, grad_query, diagonal=None):
+            k_at = pl.multiple_of(step * KT, KT)
+            block = kv[pl.ds(k_at, KT), :]
+            block_t = kvt[:HEAD_DIM, pl.ds(k_at, KT)]
+            start = 0 if diagonal is None else diagonal
+            grad_probs = [
+                jnp.dot(block, grad_t[tile], preferred_element_type=F32)
+                for tile in range(start, tiles)
             ]
+            results = list(grad_query)
+            shares = []
+            for tile in range(start, tiles):
+                factor = jnp.exp(tops[pl.ds(step, 1), tile * QT : (tile + 1) * QT] - log_rows[tile])
+                probs = held[pl.ds(k_at, KT), tile * QT : (tile + 1) * QT].astype(F32) * factor
+                grad_scores = (probs * (grad_probs[tile - start] - delta[tile])).astype(BF)
+                shares.append(
+                    jnp.dot(grad_scores, only_query[tile], preferred_element_type=F32)
+                    + jnp.dot(probs.astype(BF), only_grad[tile], preferred_element_type=F32)
+                )
+                results[tile] = grad_query[tile] + jnp.dot(
+                    block_t, grad_scores, preferred_element_type=F32
+                )
+            dkv[pl.ds(k_at, KT), :] += sum(shares[1:], shares[0])
+            return tuple(results)
+
+        grad_query = tuple(jnp.zeros((HEAD_DIM, QT), F32) for _ in range(tiles))
+        grad_query = lax.fori_loop(0, full, backward, grad_query)
+        for tile in range(tiles):
+            grad_query = backward(full + tile, grad_query, tile)
+        for tile in range(tiles):
+            result = jnp.concatenate([grad_query[tile] * (HEAD_DIM**-0.5), mixed[tile]], axis=0)
+            result = result.T.astype(BF)
+            for piece in range(QT // ROW):
+                out[tile * (QT // ROW) + piece, chunks + part] = result[
+                    piece * ROW : (piece + 1) * ROW
+                ]
         return carry
 
-    lax.fori_loop(0, 2 * tiles, one_tile, 0)
-
-    def store_keys(index, carry):
-        source, place = index // chunks, index % chunks
-        out[source, place] = dkv[pl.ds(key_place(source, place), ROW), :].astype(BF)
+    lax.fori_loop(0, 2, one_part, 0)
+
+    def store_keys(place, carry):
+        at = key_place(place)
+        for source in range(sources):
+            out[source, place] = dkv[pl.ds(at + source * ROW, ROW), :].astype(BF)
         return carry
 
-    lax.fori_loop(0, sources * chunks, store_keys, 0)
+    lax.fori_loop(0, chunks, store_keys, 0)
 
 
 def attend(message, which):
@@ -158,6 +198,8 @@
             pltpu.VMEM((wide, queries), BF),
             pltpu.VMEM((wide, queries), BF),
             pltpu.VMEM((keys, wide), F32),
+            pltpu.VMEM((keys, sources * ROW), BF),
+            pltpu.VMEM((keys // KT, sources * ROW), F32),
         ],
         compiler_params=pltpu.CompilerParams(vmem_limit_bytes=48 * 1024 * 1024),
         cost_estimate=pl.CostEstimate(
@@ -391,7 +433,7 @@
     )(which, ans, table, cosine, sine, w_joined, w_out, first, scaled, grads, feed, second)
 
 
-def settle_kernel(which, mine, other, joined, up, down, out, vectors):
+def settle_kernel(which, mine, other, joined, up, down, out, vectors, joined_bias, *norms):
     shard_rows, wide = joined.shape[0], 2 * HEAD_DIM
     planes = up.shape[1] // 1024
     up_cols = up.shape[1] // (2 * planes)
@@ -430,7 +472,13 @@
         start = 2 * side + half
         half = out.shape[0] // 2
         out[core * half : (core + 1) * half, :] = source[start : start + half]
-    vectors[...] = pltpu.roll(total, HEAD_DIM, 1)
+    total = pltpu.roll(total, HEAD_DIM, 1)
+    vectors[...] = total
+    turned = jnp.concatenate([total] * (wide // shard_rows), axis=0).T
+    joined_bias[...] = turned[5:8, :shard_rows]
+    for i, norm in enumerate(norms):
+        row = min(i, 4)
+        norm[...] = turned[row : row + 1, :shard_rows]
 
 
 def settle(which, mine, other, shapes):
@@ -641,8 +689,8 @@
         arrived, up_grad.astype(BF), split_rows(down_grad, half_down), feed, grad_second
     )
     up_arrived = send_columns(up_grad)
+    attended, up_arrived, down_rows = pin(attend(arrived, which), up_arrived, down_rows)
     down_sum = lax.psum_scatter(down_rows, PLANE, scatter_dimension=0, tiled=False)
-    attended, up_arrived = pin(attend(arrived, which), up_arrived)
     answered = exchange(attended, PLANE)
 
     block_sum, grad_scaled, joined_grad, out_grad, sums = back(
@@ -660,7 +708,7 @@
         grad_second,
     )
     out_grad = out_grad.reshape(2, 2, HEAD_DIM, width)[:, 1].reshape(head_cols, width)
-    out_arrived = exchange(split_rows(out_grad, half_out), PLANE)
+    out_rows = split_rows(out_grad, half_out)
 
     def other_core(total):
         total = total.reshape(2, planes, rows, width)
@@ -697,10 +745,10 @@
     columns = joined_grad + jnp.pad(
         vectors, ((0, 0), (side, joined_grad.shape[1] - side - n_vectors))
     )
-    columns, out_arrived = pin(columns.astype(BF), out_arrived)
-    columns = send_columns(columns)
-    grad_scaled, columns, down_sum, *block_moved = pin(
-        grad_scaled, columns, down_sum, *block_moved
+    columns, out_rows = pin(send_columns(columns.astype(BF)), out_rows)
+    out_arrived = exchange(out_rows, PLANE)
+    grad_scaled, columns, out_arrived, down_sum, *block_moved = pin(
+        grad_scaled, columns, out_arrived, down_sum, *block_moved
     )
     grad_scaled = exchange(grad_scaled, "y")
 
@@ -718,7 +766,15 @@
     far = lax.ppermute(part.astype(BF), "zh", [(0, 1), (1, 0)])
     far, grad_scaled = pin(far, grad_scaled)
     part = part + far.astype(F32)
-    joined_weight_grad, up_weight_grad, down_weight_grad, output_weight_grad, vectors = settle(
+    (
+        joined_weight_grad,
+        up_weight_grad,
+        down_weight_grad,
+        output_weight_grad,
+        vectors,
+        joined_bias_grad,
+        *norms,
+    ) = settle(
         which,
         part,
         core_swap(part),
@@ -728,8 +784,12 @@
             down_weight.shape,
             output_weight.shape,
             (shard_rows, 2 * HEAD_DIM),
-        ),
-    )
+            joined_bias.shape[::-1],
+        )
+        + ((1, shard_rows),) * 6,
+    )
+    joined_bias_grad = jnp.transpose(joined_bias_grad)
+    norms = [norm.reshape(shard_rows) for norm in norms]
     grad_scaled = jnp.sum(grad_scaled.astype(F32), axis=0)
 
     for block in block_moved:
@@ -745,18 +805,15 @@
     return (
         block_out,
         input_grad,
-        vectors[:, 0],
-        vectors[:, 1],
-        vectors[:, 2],
-        vectors[:, 3],
+        *norms[:4],
         joined_weight_grad,
-        vectors[:, 5:8],
+        joined_bias_grad,
         output_weight_grad,
-        vectors[:, 4],
+        norms[4],
         up_weight_grad,
         vectors[:, 8:12].reshape(wide_rows),
         down_weight_grad,
-        vectors[:, 4],
+        norms[5],
     )
 
 

time: 371 us -> 348 us (0.938)
  Pallas kernels: 82.1 us -> 67.3 us
  waiting for transfers between devices: 132 us -> 128 us
    pallas_call x1, Pallas kernels: 59.4 us -> 44.6 us  [attend(): pl.pallas_call(attention_kernel, out_shape=jax.ShapeDtypeStruct(message.s...]
    ppermute x3, waiting for transfers between devices: 15.8 us -> 9.48 us  [ring_move(): lax.ppermute(values, names, [(i, (i + shift) % size) for i in range(size)])]
    unnamed x75 -> x81, local copies, waits for them, and re-layouts: 8.36 us -> 8.03 us
  transfers between devices with their start and end apart: 21 -> 21, of which waited for: 11 -> 11; matrix products, arithmetic and copies ran while one was open for 16% -> 17% of each run, Pallas kernels for 19% -> 16%
where the time goes in v2:
time: 348 us; the launch traced here: 346 us
  waiting for transfers between devices  128 us (37%)
  Pallas kernels  67.3 us (19%)
  starting transfers between devices  59.6 us (17%)
  other arithmetic  27.8 us (8%)
  local copies, waits for them, and re-layouts  27.2 us (8%)
  matrix products  21.6 us (6%)
  between operations  14.8 us (4%)
    all_to_all x8, waiting for transfers between devices, exchange(): lax.all_to_all(values, names, split_axis=0, concat_axis=0, tiled=True)  79.7 us
    all_to_all x8, starting transfers between devices, exchange(): lax.all_to_all(values, names, split_axis=0, concat_axis=0, tiled=True)  45.2 us
    pallas_call x1, Pallas kernels, attend(): pl.pallas_call(attention_kernel, out_shape=jax.ShapeDtypeStruct(message.s...  44.6 us
    all_gather x1, waiting for transfers between devices, per_device(): rows_half = lax.all_gather(rows_half, PLANE, axis=0, tiled=False)  27.8 us
    pallas_call x1, Pallas kernels, back(): pl.pallas_call(back_kernel, grid=(tokens // rows,), out_shape=(jax.ShapeD...  11.7 us
    ppermute x3, waiting for transfers between devices, ring_move(): lax.ppermute(values, names, [(i, (i + shift) % size) for i in range(size)])  9.48 us
    ppermute x7, starting transfers between devices, core_swap(): return lax.ppermute(values, 'c', [(0, 1), (1, 0)])  9.46 us
    pallas_call x1, Pallas kernels, front(): pl.pallas_call(front_kernel, grid=(steps,), out_shape=(jax.ShapeDtypeStru...  9.15 us
  transfers between devices with their start and end apart: 21, of which 11 were waited for; matrix products, arithmetic and copies ran while one was open for 17% of the time, Pallas kernels for 16%

profile of v2, /device:TPU:1, one launch (start us, length us, event | category | flops | bytes accessed | tf_op | source)
XLA Modules:
  0.0 346.3 jit_solution(12719050710299049582)
XLA Ops:
  11.4 5.2 %all-to-all-start = ((bf16[4,272,1024]{2,1,0:T(8,128)(2,1)}), bf16[4,272,1024]{2,1,0:T(8,128)(2,1)}, u32[]{:S(2)}, u32[]{:S(2)}) async-start(bf16[4,272,1024]{2,1,0:T(8,128)(2,1)} %broadcast_in_dim.10), calls=%async_computation | async-start | bytes 4456448 | tf_op jit(solution)/shard_map/all_to_all | solution.py:497
  19.5 24.4 %all-to-all-done.own = bf16[4,272,1024]{2,1,0:T(8,128)(2,1)} async-done(((bf16[4,272,1024]{2,1,0:T(8,128)(2,1)}), bf16[4,272,1024]{2,1,0:T(8,128)(2,1)}, u32[]{:S(2)}, u32[]{:S(2)}) %all-to-all-start) | async-done | bytes 2228256 | tf_op jit(solution)/shard_map/all_to_all | solution.py:497
  45.6 6.4 %all-to-all-start.1 = ((bf16[32,32,1024]{2,1,0:T(8,128)(2,1)}), bf16[32,32,1024]{2,1,0:T(8,128)(2,1)S(1)}, u32[]{:S(2)}, u32[]{:S(2)}) async-start(bf16[32,32,1024]{2,1,0:T(8,128)(2,1)} %bitcast.17), calls=%async_computation.1 | async-start | bytes 4194304 | tf_op jit(solution)/shard_map/all_to_all | solution.py:497
  54.0 27.8 %all-gather.3.cloned.1.call-done = bf16[640,1024]{1,0:T(8,128)(2,1)} async-done(((bf16[80,1024]{1,0:T(8,128)(2,1)}), bf16[640,1024]{1,0:T(8,128)(2,1)}) %all-gather.3.cloned.1.call-update) | async-done | bytes 1310736 | tf_op jit(solution)/shard_map/all_gather | solution.py:617
  98.3 9.1 %front.1 = (bf16[8,10,128,128]{3,2,1,0:T(8,128)(2,1)}, bf16[1024,1024]{1,0:T(8,128)(2,1)S(1)}, bf16[1024,1024]{1,0:T(8,128)(2,1)}, f32[1024,1024]{1,0:T(8,128)}, bf16[1024,1024]{1,0:T(8,128)(2,1)}) custom-call(s32[2]{0:T(128)S(1)} %pad_add_fusion.which, bf16[4,272,1024]{2,1,0:T(8,128)(2,1)} %all-to-all-done.own, ...), custom_call_target="tpu_custom_call" | custom-call | flops 1610612736 | bytes 25165824 | tf_op jit(solution)/shard_map/front/pallas_call | solution.py:277
  108.8 6.7 %all-to-all-start.2 = ((bf16[8,10,128,128]{3,2,1,0:T(8,128)(2,1)}), bf16[8,10,128,128]{3,2,1,0:T(8,128)(2,1)}, u32[]{:S(2)}, u32[]{:S(2)}) async-start(bf16[8,10,128,128]{3,2,1,0:T(8,128)(2,1)} %get-tuple-element.59), calls=%async_computation.2 | async-start | bytes 5242880 | tf_op jit(solution)/shard_map/all_to_all | solution.py:497
  115.6 3.2 fusion.10
  118.8 6.0 %convert_reduce_fusion.4 = (f32[512]{0:T(512)S(1)}, bf16[1024,512]{1,0:T(8,128)(2,1)S(1)}, f32[1024,512]{1,0:T(8,128)S(1)}) fusion(f32[1024,512]{1,0:T(8,128)S(1)} %fusion.10, f32[512]{0:T(512)S(1)} %dynamic_slice.60, bf16[1024,1024]{1,0:T(8,128)(2,1)S(1)} %copy-done.8, bf16[512,1024]{1,0:T(8,128)(2,1)S(1)} %bitcast.151), kind=kOutput, calls=%fused_computation.11 | convolution fusion | flops 1113062912 | bytes 8392704 | tf_op jit(solution)/shard_map/td,fd->tf/dot_general | solution.py:670
  127.5 3.3 fusion.44.feed
  130.8 2.3 convolution_convert_fusion.1
  133.1 3.3 fusion.8.second
  137.7 15.9 %all-to-all-done.2.msg = bf16[8,10,128,128]{3,2,1,0:T(8,128)(2,1)} async-done(((bf16[8,10,128,128]{3,2,1,0:T(8,128)(2,1)}), bf16[8,10,128,128]{3,2,1,0:T(8,128)(2,1)}, u32[]{:S(2)}, u32[]{:S(2)}) %all-to-all-start.2) | async-done | bytes 2621472 | tf_op jit(solution)/shard_map/all_to_all | solution.py:497
  153.6 6.3 %all-to-all-start.3 = ((bf16[32,32,512]{2,1,0:T(8,128)(2,1)}), bf16[32,32,512]{2,1,0:T(8,128)(2,1)}, u32[]{:S(2)}, u32[]{:S(2)}) async-start(bf16[32,32,512]{2,1,0:T(8,128)(2,1)} %bitcast.153), calls=%async_computation.3 | async-start | bytes 2097152 | tf_op jit(solution)/shard_map/all_to_all | solution.py:497
  159.9 44.6 %attention.1 = bf16[8,10,128,128]{3,2,1,0:T(8,128)(2,1)S(1)} custom-call(s32[2]{0:T(128)S(1)} %pad_add_fusion.which, bf16[8,10,128,128]{3,2,1,0:T(8,128)(2,1)} %all-to-all-done.2.msg), custom_call_target="tpu_custom_call" | custom-call | flops 8455716864 | bytes 5242880 | tf_op jit(solution)/shard_map/attention/pallas_call | solution.py:186
  206.0 4.7 %all-to-all-start.4 = ((bf16[8,10,128,128]{3,2,1,0:T(8,128)(2,1)}), bf16[8,10,128,128]{3,2,1,0:T(8,128)(2,1)}, u32[]{:S(2)}, u32[]{:S(2)}) async-start(bf16[8,10,128,128]{3,2,1,0:T(8,128)(2,1)} %copy-done.2), calls=%async_computation.4 | async-start | bytes 5242880 | tf_op jit(solution)/shard_map/all_to_all | solution.py:497
  213.0 34.0 %all-to-all-done.4.ans = bf16[8,10,128,128]{3,2,1,0:T(8,128)(2,1)} async-done(((bf16[8,10,128,128]{3,2,1,0:T(8,128)(2,1)}), bf16[8,10,128,128]{3,2,1,0:T(8,128)(2,1)}, u32[]{:S(2)}, u32[]{:S(2)}) %all-to-all-start.4) | async-done | bytes 2621472 | tf_op jit(solution)/shard_map/all_to_all | solution.py:497
  247.0 11.7 %back.1 = (bf16[1024,1024]{1,0:T(8,128)(2,1)S(1)}, bf16[1024,1024]{1,0:T(8,128)(2,1)}, f32[1024,512]{1,0:T(8,128)}, f32[256,1024]{1,0:T(8,128)S(1)}, f32[8,1024]{1,0:T(8,128)S(1)}) custom-call(s32[2]{0:T(128)S(1)} %pad_add_fusion.which, bf16[8,10,128,128]{3,2,1,0:T(8,128)(2,1)} %all-to-all-done.4.ans, f32[16,1024]{1,0:T(8,128)S(1)} %copy.104.table, ...), custom_call_target="tpu_custom_call" | custom-call | flops 3221225472 | bytes 25165824 | tf_op jit(solution)/shard_map/back/pallas_call | solution.py:407
  261.7 3.1 add_convert_fusion
  264.8 8.7 %all-to-all-start.5 = ((bf16[32,32,512]{2,1,0:T(8,128)(2,1)}), bf16[32,32,512]{2,1,0:T(8,128)(2,1)}, u32[]{:S(2)}, u32[]{:S(2)}) async-start(bf16[32,32,512]{2,1,0:T(8,128)(2,1)} %bitcast.135), calls=%async_computation.5 | async-start | bytes 2097152 | tf_op jit(solution)/shard_map/all_to_all | solution.py:497
  273.5 3.8 %fusion.39 = (bf16[512,1024]{1,0:T(8,128)(2,1)}, bf16[512,1024]{1,0:T(8,128)(2,1)}, bf16[512,1024]{1,0:T(8,128)(2,1)}, bf16[512,1024]{1,0:T(8,128)(2,1)}) fusion(bf16[1024,1024]{1,0:T(8,128)(2,1)S(1)} %copy-done.5, bf16[1024,1024]{1,0:T(8,128)(2,1)} %get-tuple-element.71), kind=kLoop, calls=%fused_computation.131 | loop fusion | bytes 8388608 | tf_op jit(solution)/shard_map/slice | solution.py:715
  281.3 2.1 collective-permute-done.5
  284.2 5.3 %all-to-all-done.5 = bf16[32,32,512]{2,1,0:T(8,128)(2,1)} async-done(((bf16[32,32,512]{2,1,0:T(8,128)(2,1)}), bf16[32,32,512]{2,1,0:T(8,128)(2,1)}, u32[]{:S(2)}, u32[]{:S(2)}) %all-to-all-start.5) | async-done | bytes 1048608 | tf_op jit(solution)/shard_map/all_to_all | solution.py:497
  289.5 3.4 all-to-all-start.6
  298.5 2.5 fusion.1
  301.0 2.4 collective-permute-done.8
  303.4 5.0 %collective-permute-done.7 = bf16[128,1024]{1,0:T(8,128)(2,1)S(1)} collective-permute-done((bf16[128,1024]{1,0:T(8,128)(2,1)S(1)}, bf16[128,1024]{1,0:T(8,128)(2,1)S(1)}, u32[]{:S(2)}, u32[]{:S(2)}) %collective-permute-start.7) | collective-permute-done | bytes 262176 | tf_op jit(solution)/shard_map/ppermute | solution.py:509
  308.5 2.0 collective-permute-done.6
  311.2 3.8 %all-to-all-start.7 = ((bf16[4,128,1024]{2,1,0:T(8,128)(2,1)}), bf16[4,128,1024]{2,1,0:T(8,128)(2,1)S(1)}, u32[]{:S(2)}, u32[]{:S(2)}) async-start(bf16[4,128,1024]{2,1,0:T(8,128)(2,1)} %fusion.1), calls=%async_computation.8 | async-start | bytes 2097152 | tf_op jit(solution)/shard_map/all_to_all | solution.py:497
  318.4 2.9 collective-permute-start.9
  322.0 7.6 %collective-permute-done.9 = bf16[208,1024]{1,0:T(8,128)(2,1)} collective-permute-done((bf16[208,1024]{1,0:T(8,128)(2,1)}, bf16[208,1024]{1,0:T(8,128)(2,1)}, u32[]{:S(2)}, u32[]{:S(2)}) %collective-permute-start.9) | collective-permute-done | bytes 426016 | tf_op jit(solution)/shard_map/ppermute | solution.py:766
  331.4 3.0 collective-permute-start.10
  334.7 2.2 fusion.20
  (206 shorter events, 58.8 us)
Async XLA Ops:
  7.2 9.4 %copy-start = (bf16[128,1024]{1,0:T(8,128)(2,1)S(1)}, bf16[128,1024]{1,0:T(8,128)(2,1)}, u32[]{:S(2)}) copy-start(bf16[128,1024]{1,0:T(8,128)(2,1)} %param.29) | copy-start | bytes 786436
  11.4 6.6 %copy-start.36 = (bf16[128]{0:T(256)(128)(2,1)S(1)}, bf16[128]{0:T(256)(128)(2,1)}, u32[]{:S(2)}) copy-start(bf16[128]{0:T(256)(128)(2,1)} %param.28) | copy-start | bytes 772
  11.4 6.7 %copy-start.37 = (bf16[32]{0:T(256)(128)(2,1)S(1)}, bf16[32]{0:T(256)(128)(2,1)}, u32[]{:S(2)}) copy-start(bf16[32]{0:T(256)(128)(2,1)} %param.30) | copy-start | bytes 196
  11.4 6.8 %copy-start.26 = (bf16[32,4096]{1,0:T(8,128)(2,1)S(1)}, bf16[32,4096]{1,0:T(8,128)(2,1)}, u32[]{:S(2)}) copy-start(bf16[32,4096]{1,0:T(8,128)(2,1)} %param.27) | copy-start | bytes 786436
  11.4 32.6 %all-to-all-start = ((bf16[4,272,1024]{2,1,0:T(8,128)(2,1)}), bf16[4,272,1024]{2,1,0:T(8,128)(2,1)}, u32[]{:S(2)}, u32[]{:S(2)}) async-start(bf16[4,272,1024]{2,1,0:T(8,128)(2,1)} %broadcast_in_dim.10), calls=%async_computation | async-start | bytes 4456448 | tf_op jit(solution)/shard_map/all_to_all | solution.py:497
  16.6 65.2 %all-gather.3.cloned.1.call-start = ((), (), s32[]{:S(2)}) async-start(), calls=%async_computation.10 | async-start | bytes 1474560 | tf_op jit(solution)/shard_map/all_gather | solution.py:617
  45.6 44.1 %all-to-all-start.1 = ((bf16[32,32,1024]{2,1,0:T(8,128)(2,1)}), bf16[32,32,1024]{2,1,0:T(8,128)(2,1)S(1)}, u32[]{:S(2)}, u32[]{:S(2)}) async-start(bf16[32,32,1024]{2,1,0:T(8,128)(2,1)} %bitcast.17), calls=%async_computation.1 | async-start | bytes 4194304 | tf_op jit(solution)/shard_map/all_to_all | solution.py:497
  52.0 43.3 %collective-permute-start = (bf16[4,272,1024]{2,1,0:T(8,128)(2,1)}, bf16[4,272,1024]{2,1,0:T(8,128)(2,1)}, u32[]{:S(2)}, u32[]{:S(2)}) collective-permute-start(bf16[4,272,1024]{2,1,0:T(8,128)(2,1)} %all-to-all-done.own), channel_id=1, source_target_pairs={{0,32},{32,0},{1,33},{33,1},{2,34},{34,2},{3,35},{35,3},{4,36},{36... | collective-permute-start | bytes 6684680 | tf_op jit(solution)/shard_map/ppermute | solution.py:501
  83.7 3.5 %collective-permute-start.1 = (bf16[4,80,1024]{2,1,0:T(8,128)(2,1)}, bf16[4,80,1024]{2,1,0:T(8,128)(2,1)}, u32[]{:S(2)}, u32[]{:S(2)}) collective-permute-start(bf16[4,80,1024]{2,1,0:T(8,128)(2,1)} %constant_dynamic-slice_fusion), channel_id=1, source_target_pairs={{0,32},{32,0},{1,33},{33,1},{2,34},{34,2},{3,35},{35,3},{4,36},{36... | collective-permute-start | bytes 1966088 | tf_op jit(solution)/shard_map/ppermute | solution.py:501
  108.8 44.8 %all-to-all-start.2 = ((bf16[8,10,128,128]{3,2,1,0:T(8,128)(2,1)}), bf16[8,10,128,128]{3,2,1,0:T(8,128)(2,1)}, u32[]{:S(2)}, u32[]{:S(2)}) async-start(bf16[8,10,128,128]{3,2,1,0:T(8,128)(2,1)} %get-tuple-element.59), calls=%async_computation.2 | async-start | bytes 5242880 | tf_op jit(solution)/shard_map/all_to_all | solution.py:497
  126.7 9.7 %collective-permute-start.2 = (bf16[4,64,1024]{2,1,0:T(8,128)(2,1)S(1)}, bf16[4,64,1024]{2,1,0:T(8,128)(2,1)S(1)}, u32[]{:S(2)}, u32[]{:S(2)}) collective-permute-start(bf16[4,64,1024]{2,1,0:T(8,128)(2,1)S(1)} %dynamic-slice_bitcast_fusion), channel_id=1, source_target_pairs={{0,32},{32,0},{1,33},{33,1},{2,34},{34,2},{3,35},{35,3},{4,36},{36... | collective-permute-start | bytes 1572872 | tf_op jit(solution)/shard_map/ppermute | solution.py:501
  153.6 52.4 %all-to-all-start.3 = ((bf16[32,32,512]{2,1,0:T(8,128)(2,1)}), bf16[32,32,512]{2,1,0:T(8,128)(2,1)}, u32[]{:S(2)}, u32[]{:S(2)}) async-start(bf16[32,32,512]{2,1,0:T(8,128)(2,1)} %bitcast.153), calls=%async_computation.3 | async-start | bytes 2097152 | tf_op jit(solution)/shard_map/all_to_all | solution.py:497
  206.0 41.0 %all-to-all-start.4 = ((bf16[8,10,128,128]{3,2,1,0:T(8,128)(2,1)}), bf16[8,10,128,128]{3,2,1,0:T(8,128)(2,1)}, u32[]{:S(2)}, u32[]{:S(2)}) async-start(bf16[8,10,128,128]{3,2,1,0:T(8,128)(2,1)} %copy-done.2), calls=%async_computation.4 | async-start | bytes 5242880 | tf_op jit(solution)/shard_map/all_to_all | solution.py:497
  210.6 90.4 %reduce-scatter.2.cloned.1.call-start = ((), (), s32[]{:S(2)}) async-start(), calls=%async_computation.9 | async-start | bytes 1179648 | tf_op jit(solution)/shard_map/reduce_scatter | solution.py:693
  261.7 11.8 %copy-start.5 = (bf16[1024,1024]{1,0:T(8,128)(2,1)S(1)}, bf16[1024,1024]{1,0:T(8,128)(2,1)}, u32[]{:S(2)}) copy-start(bf16[1024,1024]{1,0:T(8,128)(2,1)} %copy-done.4) | copy-start | bytes 6291460
  264.8 24.7 %all-to-all-start.5 = ((bf16[32,32,512]{2,1,0:T(8,128)(2,1)}), bf16[32,32,512]{2,1,0:T(8,128)(2,1)}, u32[]{:S(2)}, u32[]{:S(2)}) async-start(bf16[32,32,512]{2,1,0:T(8,128)(2,1)} %bitcast.135), calls=%async_computation.5 | async-start | bytes 2097152 | tf_op jit(solution)/shard_map/all_to_all | solution.py:497
  273.5 7.0 %copy-start.7 = (f32[256,1024]{1,0:T(8,128)S(1)}, f32[256,1024]{1,0:T(8,128)}, u32[]{:S(2)}) copy-start(f32[256,1024]{1,0:T(8,128)} %copy-done.6) | copy-start | bytes 3145732
  277.3 15.6 %collective-permute-start.3 = (bf16[4,128,1024]{2,1,0:T(8,128)(2,1)}, bf16[4,128,1024]{2,1,0:T(8,128)(2,1)S(1)}, u32[]{:S(2)}, u32[]{:S(2)}) collective-permute-start(bf16[4,128,1024]{2,1,0:T(8,128)(2,1)} %bitcast.35), channel_id=1, source_target_pairs={{0,32},{32,0},{1,33},{33,1},{2,34},{34,2},{3,35},{35,3},{4,36},{36... | collective-permute-start | bytes 3145736 | tf_op jit(solution)/shard_map/ppermute | solution.py:501
  280.5 13.4 %copy-start.13 = (bf16[512,1024]{1,0:T(8,128)(2,1)S(1)}, bf16[512,1024]{1,0:T(8,128)(2,1)}, u32[]{:S(2)}) copy-start(bf16[512,1024]{1,0:T(8,128)(2,1)} %get-tuple-element.111) | copy-start | bytes 3145732
  280.6 17.9 %collective-permute-start.4 = (bf16[4,128,1024]{2,1,0:T(8,128)(2,1)}, bf16[4,128,1024]{2,1,0:T(8,128)(2,1)}, u32[]{:S(2)}, u32[]{:S(2)}) collective-permute-start(bf16[4,128,1024]{2,1,0:T(8,128)(2,1)} %bitcast.38), channel_id=1, source_target_pairs={{0,32},{32,0},{1,33},{33,1},{2,34},{34,2},{3,35},{35,3},{4,36},{36... | collective-permute-start | bytes 3145736 | tf_op jit(solution)/shard_map/ppermute | solution.py:501
  280.8 2.7 collective-permute-start.5
  281.3 36.3 %copy-start.15 = (f32[2,32,512]{2,1,0:T(8,128)}, f32[2,32,512]{2,1,0:T(8,128)S(1)}, u32[]{:S(2)}) copy-start(f32[2,32,512]{2,1,0:T(8,128)S(1)} %get-tuple-element.128) | copy-start | bytes 393220
  289.5 11.5 %all-to-all-start.6 = ((bf16[8,16,1024]{2,1,0:T(8,128)(2,1)}), bf16[8,16,1024]{2,1,0:T(8,128)(2,1)S(1)}, u32[]{:S(2)}, u32[]{:S(2)}) async-start(bf16[8,16,1024]{2,1,0:T(8,128)(2,1)} %pad_maximum_fusion.5), calls=%async_computation.6 | async-start | bytes 524288 | tf_op jit(solution)/shard_map/all_to_all | solution.py:497
  296.4 7.0 %collective-permute-start.8 = (bf16[128,1024]{1,0:T(8,128)(2,1)}, bf16[128,1024]{1,0:T(8,128)(2,1)S(1)}, u32[]{:S(2)}, u32[]{:S(2)}) collective-permute-start(bf16[128,1024]{1,0:T(8,128)(2,1)} %get-tuple-element.118), channel_id=1, source_target_pairs={{0,16},{8,24},{16,0},{24,8},{1,17},{9,25},{17,1},{25,9},{2,18},{10... | collective-permute-start | bytes 786440 | tf_op jit(solution)/shard_map/ppermute | solution.py:509
  296.9 11.6 %collective-permute-start.7 = (bf16[128,1024]{1,0:T(8,128)(2,1)S(1)}, bf16[128,1024]{1,0:T(8,128)(2,1)S(1)}, u32[]{:S(2)}, u32[]{:S(2)}) collective-permute-start(bf16[128,1024]{1,0:T(8,128)(2,1)S(1)} %get-tuple-element.119), channel_id=1, source_target_pairs={{0,24},{8,0},{16,8},{24,16},{1,25},{9,1},{17,9},{25,17},{2,26},{10... | collective-permute-start | bytes 786440 | tf_op jit(solution)/shard_map/ppermute | solution.py:509
  298.5 12.0 %collective-permute-start.6 = (bf16[128,1024]{1,0:T(8,128)(2,1)S(1)}, bf16[128,1024]{1,0:T(8,128)(2,1)S(1)}, u32[]{:S(2)}, u32[]{:S(2)}) collective-permute-start(bf16[128,1024]{1,0:T(8,128)(2,1)S(1)} %get-tuple-element.120), channel_id=1, source_target_pairs={{0,8},{8,16},{16,24},{24,0},{1,9},{9,17},{17,25},{25,1},{2,10},{10... | collective-permute-start | bytes 786440 | tf_op jit(solution)/shard_map/ppermute | solution.py:509
  301.0 10.2 %copy-start.19 = (bf16[8,16,1024]{2,1,0:T(8,128)(2,1)}, bf16[8,16,1024]{2,1,0:T(8,128)(2,1)S(1)}, u32[]{:S(2)}) copy-start(bf16[8,16,1024]{2,1,0:T(8,128)(2,1)S(1)} %all-to-all-done.6) | copy-start | bytes 786436
  303.4 7.8 %copy-start.23 = (bf16[128,1024]{1,0:T(8,128)(2,1)}, bf16[128,1024]{1,0:T(8,128)(2,1)S(1)}, u32[]{:S(2)}) copy-start(bf16[128,1024]{1,0:T(8,128)(2,1)S(1)} %collective-permute-done.8) | copy-start | bytes 786436
  311.2 18.4 %all-to-all-start.7 = ((bf16[4,128,1024]{2,1,0:T(8,128)(2,1)}), bf16[4,128,1024]{2,1,0:T(8,128)(2,1)S(1)}, u32[]{:S(2)}, u32[]{:S(2)}) async-start(bf16[4,128,1024]{2,1,0:T(8,128)(2,1)} %fusion.1), calls=%async_computation.8 | async-start | bytes 2097152 | tf_op jit(solution)/shard_map/all_to_all | solution.py:497
  318.4 11.2 %collective-permute-start.9 = (bf16[208,1024]{1,0:T(8,128)(2,1)}, bf16[208,1024]{1,0:T(8,128)(2,1)}, u32[]{:S(2)}, u32[]{:S(2)}) collective-permute-start(bf16[208,1024]{1,0:T(8,128)(2,1)} %fusion.26), channel_id=1, source_target_pairs={{0,64},{64,0},{1,65},{65,1},{2,66},{66,2},{3,67},{67,3},{4,68},{68... | collective-permute-start | bytes 1277960 | tf_op jit(solution)/shard_map/ppermute | solution.py:766
  322.0 12.6 %copy-start.14 = (bf16[128,1024]{1,0:T(8,128)(2,1)S(1)}, bf16[128,1024]{1,0:T(8,128)(2,1)}, u32[]{:S(2)}) copy-start(bf16[128,1024]{1,0:T(8,128)(2,1)} %param.31) | copy-start | bytes 786436
  331.4 5.5 %collective-permute-start.10 = (f32[208,1024]{1,0:T(8,128)S(1)}, f32[208,1024]{1,0:T(8,128)S(1)}, u32[]{:S(2)}, u32[]{:S(2)}) collective-permute-start(f32[208,1024]{1,0:T(8,128)S(1)} %convert_add_fusion.2.mine), channel_id=1, source_target_pairs={{0,32},{32,0},{1,33},{33,1},{2,34},{34,2},{3,35},{35,3},{4,36},{36... | collective-permute-start | bytes 2555912 | tf_op jit(solution)/shard_map/ppermute | solution.py:501
  (29 other events, 106.3 us)
Sparse Core Ops, SparseCore 0:
  19.6 62.0 all-gather.2
  213.8 52.2 reduce-scatter.1

commit v3 on v2

--- a/solution.py
+++ b/solution.py
@@ -636,11 +636,13 @@
 
     cosine, sine = to_lanes(jnp.cos(angles)) + keep, to_lanes(jnp.sin(angles))
 
-    own = lax.dynamic_slice_in_dim(rows_half, core * (peers // 2), peers // 2, 0)
-    far = lax.dynamic_slice_in_dim(rows_half, (1 - core) * (peers // 2), peers // 2, 0)
-    halves = jnp.stack(in_order(core, own, core_swap(far)), axis=1)
-    w_down = halves[:, :, half_out:].reshape(up_cols, width)
-    w_out = halves[:, :, :half_out].reshape(2, HEAD_DIM, width)
+    def own_rows(gathered):
+        own = lax.dynamic_slice_in_dim(gathered, core * (peers // 2), peers // 2, 0)
+        far = lax.dynamic_slice_in_dim(gathered, (1 - core) * (peers // 2), peers // 2, 0)
+        pair = jnp.stack(in_order(core, own, core_swap(far)), axis=1)
+        return pair.reshape(peers * gathered.shape[1], width)
+
+    w_out = own_rows(rows_half[:, :half_out]).reshape(2, HEAD_DIM, width)
     w_out = jnp.pad(w_out, ((0, 0), (HEAD_DIM, 0), (0, 0))).reshape(2 * head_cols, width)
 
     gain_one, gain_two = table[0], table[2]
@@ -660,6 +662,8 @@
     message, first_in, second_in, scaled, grads = front(
         which, payload, payload_far, table, bias_joined, cosine, sine, w_joined, w_out
     )
+    message, rows_half = pin(message, rows_half)
+    w_down = own_rows(rows_half[:, half_out:])
 
     arrived = exchange(message, PLANE)
 

time: 348 us -> 347 us (level)
    unnamed x81 -> x85, local copies, waits for them, and re-layouts: 8.03 us -> 10.4 us
    ppermute x7 -> x8, starting transfers between devices: 9.46 us -> 9.71 us  [core_swap(): return lax.ppermute(values, 'c', [(0, 1), (1, 0)])]
  transfers between devices with their start and end apart: 21 -> 22, of which waited for: 11 -> 11; matrix products, arithmetic and copies ran while one was open for 17% -> 16% of each run, Pallas kernels for 16% -> 16%
where the time goes in v3:
time: 347 us; the launch traced here: 345 us
  waiting for transfers between devices  125 us (36%)
  Pallas kernels  67.4 us (19%)
  starting transfers between devices  59.9 us (17%)
  local copies, waits for them, and re-layouts  29.6 us (9%)
  other arithmetic  26.7 us (8%)
  matrix products  21.6 us (6%)
  between operations  14.9 us (4%)
    all_to_all x8, waiting for transfers between devices, exchange(): lax.all_to_all(values, names, split_axis=0, concat_axis=0, tiled=True)  77.8 us
    all_to_all x8, starting transfers between devices, exchange(): lax.all_to_all(values, names, split_axis=0, concat_axis=0, tiled=True)  45.6 us
    pallas_call x1, Pallas kernels, attend(): pl.pallas_call(attention_kernel, out_shape=jax.ShapeDtypeStruct(message.s...  44.6 us
    all_gather x1, waiting for transfers between devices, per_device(): rows_half = lax.all_gather(rows_half, PLANE, axis=0, tiled=False)  27.8 us
    pallas_call x1, Pallas kernels, back(): pl.pallas_call(back_kernel, grid=(tokens // rows,), out_shape=(jax.ShapeD...  11.7 us
    unnamed x85, local copies, waits for them, and re-layouts  10.4 us
    ppermute x8, starting transfers between devices, core_swap(): return lax.ppermute(values, 'c', [(0, 1), (1, 0)])  9.71 us
    ppermute x3, waiting for transfers between devices, ring_move(): lax.ppermute(values, names, [(i, (i + shift) % size) for i in range(size)])  9.51 us
  transfers between devices with their start and end apart: 22, of which 11 were waited for; matrix products, arithmetic and copies ran while one was open for 16% of the time, Pallas kernels for 16%

profile of v3, /device:TPU:1, one launch (start us, length us, event | category | flops | bytes accessed | tf_op | source)
XLA Modules:
  0.0 345.4 jit_solution(16315381814113786556)
XLA Ops:
  11.4 5.2 %all-to-all-start = ((bf16[4,272,1024]{2,1,0:T(8,128)(2,1)}), bf16[4,272,1024]{2,1,0:T(8,128)(2,1)}, u32[]{:S(2)}, u32[]{:S(2)}) async-start(bf16[4,272,1024]{2,1,0:T(8,128)(2,1)} %broadcast_in_dim.10), calls=%async_computation | async-start | bytes 4456448 | tf_op jit(solution)/shard_map/all_to_all | solution.py:497
  19.5 24.4 %all-to-all-done.own = bf16[4,272,1024]{2,1,0:T(8,128)(2,1)} async-done(((bf16[4,272,1024]{2,1,0:T(8,128)(2,1)}), bf16[4,272,1024]{2,1,0:T(8,128)(2,1)}, u32[]{:S(2)}, u32[]{:S(2)}) %all-to-all-start) | async-done | bytes 2228256 | tf_op jit(solution)/shard_map/all_to_all | solution.py:497
  45.5 6.5 %all-to-all-start.1 = ((bf16[32,32,1024]{2,1,0:T(8,128)(2,1)}), bf16[32,32,1024]{2,1,0:T(8,128)(2,1)S(1)}, u32[]{:S(2)}, u32[]{:S(2)}) async-start(bf16[32,32,1024]{2,1,0:T(8,128)(2,1)} %bitcast.17), calls=%async_computation.1 | async-start | bytes 4194304 | tf_op jit(solution)/shard_map/all_to_all | solution.py:497
  54.0 27.8 %all-gather.3.cloned.1.call-done = bf16[640,1024]{1,0:T(8,128)(2,1)} async-done(((bf16[80,1024]{1,0:T(8,128)(2,1)}), bf16[640,1024]{1,0:T(8,128)(2,1)}) %all-gather.3.cloned.1.call-update) | async-done | bytes 1310736 | tf_op jit(solution)/shard_map/all_gather | solution.py:617
  91.7 9.3 %front.1 = (bf16[8,10,128,128]{3,2,1,0:T(8,128)(2,1)}, bf16[1024,1024]{1,0:T(8,128)(2,1)S(1)}, bf16[1024,1024]{1,0:T(8,128)(2,1)}, f32[1024,1024]{1,0:T(8,128)}, bf16[1024,1024]{1,0:T(8,128)(2,1)}) custom-call(s32[2]{0:T(128)S(1)} %pad_add_fusion.which, bf16[4,272,1024]{2,1,0:T(8,128)(2,1)} %all-to-all-done.own, ...), custom_call_target="tpu_custom_call" | custom-call | flops 1610612736 | bytes 25165824 | tf_op jit(solution)/shard_map/front/pallas_call | solution.py:277
  107.0 6.7 %all-to-all-start.2 = ((bf16[8,10,128,128]{3,2,1,0:T(8,128)(2,1)}), bf16[8,10,128,128]{3,2,1,0:T(8,128)(2,1)}, u32[]{:S(2)}, u32[]{:S(2)}) async-start(bf16[8,10,128,128]{3,2,1,0:T(8,128)(2,1)} %get-tuple-element.62), calls=%async_computation.2 | async-start | bytes 5242880 | tf_op jit(solution)/shard_map/all_to_all | solution.py:497
  113.8 3.2 fusion.10
  119.7 6.0 %convert_reduce_fusion.4 = (f32[512]{0:T(512)S(1)}, bf16[1024,512]{1,0:T(8,128)(2,1)S(1)}, f32[1024,512]{1,0:T(8,128)S(1)}) fusion(f32[1024,512]{1,0:T(8,128)S(1)} %fusion.10, f32[512]{0:T(512)S(1)} %dynamic_slice.66, bf16[1024,1024]{1,0:T(8,128)(2,1)S(1)} %copy-done.8, bf16[512,1024]{1,0:T(8,128)(2,1)S(1)} %bitcast.156), kind=kOutput, calls=%fused_computation.11 | convolution fusion | flops 1113062912 | bytes 8392704 | tf_op jit(solution)/shard_map/td,fd->tf/dot_general | solution.py:674
  128.1 3.3 fusion.44.feed
  131.4 2.3 convolution_convert_fusion.1
  133.7 3.4 fusion.8.second
  138.2 13.7 %all-to-all-done.2.msg = bf16[8,10,128,128]{3,2,1,0:T(8,128)(2,1)} async-done(((bf16[8,10,128,128]{3,2,1,0:T(8,128)(2,1)}), bf16[8,10,128,128]{3,2,1,0:T(8,128)(2,1)}, u32[]{:S(2)}, u32[]{:S(2)}) %all-to-all-start.2) | async-done | bytes 2621472 | tf_op jit(solution)/shard_map/all_to_all | solution.py:497
  152.0 6.7 %all-to-all-start.3 = ((bf16[32,32,512]{2,1,0:T(8,128)(2,1)}), bf16[32,32,512]{2,1,0:T(8,128)(2,1)}, u32[]{:S(2)}, u32[]{:S(2)}) async-start(bf16[32,32,512]{2,1,0:T(8,128)(2,1)} %bitcast.155), calls=%async_computation.3 | async-start | bytes 2097152 | tf_op jit(solution)/shard_map/all_to_all | solution.py:497
  158.7 44.6 %attention.1 = bf16[8,10,128,128]{3,2,1,0:T(8,128)(2,1)S(1)} custom-call(s32[2]{0:T(128)S(1)} %pad_add_fusion.which, bf16[8,10,128,128]{3,2,1,0:T(8,128)(2,1)} %all-to-all-done.2.msg), custom_call_target="tpu_custom_call" | custom-call | flops 8455716864 | bytes 5242880 | tf_op jit(solution)/shard_map/attention/pallas_call | solution.py:186
  204.8 4.7 %all-to-all-start.4 = ((bf16[8,10,128,128]{3,2,1,0:T(8,128)(2,1)}), bf16[8,10,128,128]{3,2,1,0:T(8,128)(2,1)}, u32[]{:S(2)}, u32[]{:S(2)}) async-start(bf16[8,10,128,128]{3,2,1,0:T(8,128)(2,1)} %copy-done.2), calls=%async_computation.4 | async-start | bytes 5242880 | tf_op jit(solution)/shard_map/all_to_all | solution.py:497
  211.8 34.3 %all-to-all-done.4.ans = bf16[8,10,128,128]{3,2,1,0:T(8,128)(2,1)} async-done(((bf16[8,10,128,128]{3,2,1,0:T(8,128)(2,1)}), bf16[8,10,128,128]{3,2,1,0:T(8,128)(2,1)}, u32[]{:S(2)}, u32[]{:S(2)}) %all-to-all-start.4) | async-done | bytes 2621472 | tf_op jit(solution)/shard_map/all_to_all | solution.py:497
  246.1 11.7 %back.1 = (bf16[1024,1024]{1,0:T(8,128)(2,1)S(1)}, bf16[1024,1024]{1,0:T(8,128)(2,1)}, f32[1024,512]{1,0:T(8,128)}, f32[256,1024]{1,0:T(8,128)S(1)}, f32[8,1024]{1,0:T(8,128)S(1)}) custom-call(s32[2]{0:T(128)S(1)} %pad_add_fusion.which, bf16[8,10,128,128]{3,2,1,0:T(8,128)(2,1)} %all-to-all-done.4.ans, f32[16,1024]{1,0:T(8,128)S(1)} %copy.107.table, ...), custom_call_target="tpu_custom_call" | custom-call | flops 3221225472 | bytes 25165824 | tf_op jit(solution)/shard_map/back/pallas_call | solution.py:407
  260.8 3.1 add_convert_fusion
  263.9 8.7 %all-to-all-start.5 = ((bf16[32,32,512]{2,1,0:T(8,128)(2,1)}), bf16[32,32,512]{2,1,0:T(8,128)(2,1)}, u32[]{:S(2)}, u32[]{:S(2)}) async-start(bf16[32,32,512]{2,1,0:T(8,128)(2,1)} %bitcast.139), calls=%async_computation.5 | async-start | bytes 2097152 | tf_op jit(solution)/shard_map/all_to_all | solution.py:497
  272.6 3.7 %fusion.39 = (bf16[512,1024]{1,0:T(8,128)(2,1)}, bf16[512,1024]{1,0:T(8,128)(2,1)}, bf16[512,1024]{1,0:T(8,128)(2,1)}, bf16[512,1024]{1,0:T(8,128)(2,1)}) fusion(bf16[1024,1024]{1,0:T(8,128)(2,1)S(1)} %copy-done.5, bf16[1024,1024]{1,0:T(8,128)(2,1)} %get-tuple-element.75), kind=kLoop, calls=%fused_computation.134 | loop fusion | bytes 8388608 | tf_op jit(solution)/shard_map/slice | solution.py:719
  280.4 2.1 collective-permute-done.6
  283.3 5.3 %all-to-all-done.5 = bf16[32,32,512]{2,1,0:T(8,128)(2,1)} async-done(((bf16[32,32,512]{2,1,0:T(8,128)(2,1)}), bf16[32,32,512]{2,1,0:T(8,128)(2,1)}, u32[]{:S(2)}, u32[]{:S(2)}) %all-to-all-start.5) | async-done | bytes 1048608 | tf_op jit(solution)/shard_map/all_to_all | solution.py:497
  288.6 3.4 all-to-all-start.6
  297.6 2.5 fusion.1
  300.1 2.5 collective-permute-done.9
  302.5 4.9 %collective-permute-done.8 = bf16[128,1024]{1,0:T(8,128)(2,1)S(1)} collective-permute-done((bf16[128,1024]{1,0:T(8,128)(2,1)S(1)}, bf16[128,1024]{1,0:T(8,128)(2,1)S(1)}, u32[]{:S(2)}, u32[]{:S(2)}) %collective-permute-start.8) | collective-permute-done | bytes 262176 | tf_op jit(solution)/shard_map/ppermute | solution.py:509
  307.5 2.1 collective-permute-done.7
  310.3 3.8 %all-to-all-start.7 = ((bf16[4,128,1024]{2,1,0:T(8,128)(2,1)}), bf16[4,128,1024]{2,1,0:T(8,128)(2,1)S(1)}, u32[]{:S(2)}, u32[]{:S(2)}) async-start(bf16[4,128,1024]{2,1,0:T(8,128)(2,1)} %fusion.1), calls=%async_computation.8 | async-start | bytes 2097152 | tf_op jit(solution)/shard_map/all_to_all | solution.py:497
  317.5 2.6 collective-permute-start.10
  320.8 7.9 %collective-permute-done.10 = bf16[208,1024]{1,0:T(8,128)(2,1)} collective-permute-done((bf16[208,1024]{1,0:T(8,128)(2,1)}, bf16[208,1024]{1,0:T(8,128)(2,1)}, u32[]{:S(2)}, u32[]{:S(2)}) %collective-permute-start.10) | collective-permute-done | bytes 426016 | tf_op jit(solution)/shard_map/ppermute | solution.py:770
  330.6 2.9 collective-permute-start.11
  333.8 2.2 fusion.20
  (218 shorter events, 59.2 us)
Async XLA Ops:
  7.2 9.4 %copy-start = (bf16[128,1024]{1,0:T(8,128)(2,1)S(1)}, bf16[128,1024]{1,0:T(8,128)(2,1)}, u32[]{:S(2)}) copy-start(bf16[128,1024]{1,0:T(8,128)(2,1)} %param.29) | copy-start | bytes 786436
  11.4 6.8 %copy-start.28 = (bf16[32,4096]{1,0:T(8,128)(2,1)S(1)}, bf16[32,4096]{1,0:T(8,128)(2,1)}, u32[]{:S(2)}) copy-start(bf16[32,4096]{1,0:T(8,128)(2,1)} %param.27) | copy-start | bytes 786436
  11.4 32.5 %all-to-all-start = ((bf16[4,272,1024]{2,1,0:T(8,128)(2,1)}), bf16[4,272,1024]{2,1,0:T(8,128)(2,1)}, u32[]{:S(2)}, u32[]{:S(2)}) async-start(bf16[4,272,1024]{2,1,0:T(8,128)(2,1)} %broadcast_in_dim.10), calls=%async_computation | async-start | bytes 4456448 | tf_op jit(solution)/shard_map/all_to_all | solution.py:497
  16.6 65.2 %all-gather.3.cloned.1.call-start = ((), (), s32[]{:S(2)}) async-start(), calls=%async_computation.10 | async-start | bytes 1474560 | tf_op jit(solution)/shard_map/all_gather | solution.py:617
  45.5 39.8 %all-to-all-start.1 = ((bf16[32,32,1024]{2,1,0:T(8,128)(2,1)}), bf16[32,32,1024]{2,1,0:T(8,128)(2,1)S(1)}, u32[]{:S(2)}, u32[]{:S(2)}) async-start(bf16[32,32,1024]{2,1,0:T(8,128)(2,1)} %bitcast.17), calls=%async_computation.1 | async-start | bytes 4194304 | tf_op jit(solution)/shard_map/all_to_all | solution.py:497
  52.0 36.7 %collective-permute-start = (bf16[4,272,1024]{2,1,0:T(8,128)(2,1)}, bf16[4,272,1024]{2,1,0:T(8,128)(2,1)}, u32[]{:S(2)}, u32[]{:S(2)}) collective-permute-start(bf16[4,272,1024]{2,1,0:T(8,128)(2,1)} %all-to-all-done.own), channel_id=1, source_target_pairs={{0,32},{32,0},{1,33},{33,1},{2,34},{34,2},{3,35},{35,3},{4,36},{36... | collective-permute-start | bytes 6684680 | tf_op jit(solution)/shard_map/ppermute | solution.py:501
  82.7 2.5 collective-permute-start.1
  91.7 10.6 %copy-start.17 = (bf16[640,1024]{1,0:T(8,128)(2,1)S(1)}, bf16[640,1024]{1,0:T(8,128)(2,1)}, u32[]{:S(2)}) copy-start(bf16[640,1024]{1,0:T(8,128)(2,1)} %all-gather.3.cloned.1.call-done) | copy-start | bytes 3932164
  104.3 12.7 %collective-permute-start.2 = (bf16[4,64,1024]{2,1,0:T(8,128)(2,1)}, bf16[4,64,1024]{2,1,0:T(8,128)(2,1)}, u32[]{:S(2)}, u32[]{:S(2)}) collective-permute-start(bf16[4,64,1024]{2,1,0:T(8,128)(2,1)} %constant_dynamic-slice_fusion), channel_id=1, source_target_pairs={{0,32},{32,0},{1,33},{33,1},{2,34},{34,2},{3,35},{35,3},{4,36},{36... | collective-permute-start | bytes 1572872 | tf_op jit(solution)/shard_map/ppermute | solution.py:501
  107.0 44.9 %all-to-all-start.2 = ((bf16[8,10,128,128]{3,2,1,0:T(8,128)(2,1)}), bf16[8,10,128,128]{3,2,1,0:T(8,128)(2,1)}, u32[]{:S(2)}, u32[]{:S(2)}) async-start(bf16[8,10,128,128]{3,2,1,0:T(8,128)(2,1)} %get-tuple-element.62), calls=%async_computation.2 | async-start | bytes 5242880 | tf_op jit(solution)/shard_map/all_to_all | solution.py:497
  127.6 9.4 %collective-permute-start.3 = (bf16[4,64,1024]{2,1,0:T(8,128)(2,1)S(1)}, bf16[4,64,1024]{2,1,0:T(8,128)(2,1)S(1)}, u32[]{:S(2)}, u32[]{:S(2)}) collective-permute-start(bf16[4,64,1024]{2,1,0:T(8,128)(2,1)S(1)} %dynamic-slice_bitcast_fusion), channel_id=1, source_target_pairs={{0,32},{32,0},{1,33},{33,1},{2,34},{34,2},{3,35},{35,3},{4,36},{36... | collective-permute-start | bytes 1572872 | tf_op jit(solution)/shard_map/ppermute | solution.py:501
  152.0 52.8 %all-to-all-start.3 = ((bf16[32,32,512]{2,1,0:T(8,128)(2,1)}), bf16[32,32,512]{2,1,0:T(8,128)(2,1)}, u32[]{:S(2)}, u32[]{:S(2)}) async-start(bf16[32,32,512]{2,1,0:T(8,128)(2,1)} %bitcast.155), calls=%async_computation.3 | async-start | bytes 2097152 | tf_op jit(solution)/shard_map/all_to_all | solution.py:497
  204.8 41.3 %all-to-all-start.4 = ((bf16[8,10,128,128]{3,2,1,0:T(8,128)(2,1)}), bf16[8,10,128,128]{3,2,1,0:T(8,128)(2,1)}, u32[]{:S(2)}, u32[]{:S(2)}) async-start(bf16[8,10,128,128]{3,2,1,0:T(8,128)(2,1)} %copy-done.2), calls=%async_computation.4 | async-start | bytes 5242880 | tf_op jit(solution)/shard_map/all_to_all | solution.py:497
  209.4 90.6 %reduce-scatter.2.cloned.1.call-start = ((), (), s32[]{:S(2)}) async-start(), calls=%async_computation.9 | async-start | bytes 1179648 | tf_op jit(solution)/shard_map/reduce_scatter | solution.py:697
  260.8 11.8 %copy-start.5 = (bf16[1024,1024]{1,0:T(8,128)(2,1)S(1)}, bf16[1024,1024]{1,0:T(8,128)(2,1)}, u32[]{:S(2)}) copy-start(bf16[1024,1024]{1,0:T(8,128)(2,1)} %copy-done.4) | copy-start | bytes 6291460
  263.9 24.7 %all-to-all-start.5 = ((bf16[32,32,512]{2,1,0:T(8,128)(2,1)}), bf16[32,32,512]{2,1,0:T(8,128)(2,1)}, u32[]{:S(2)}, u32[]{:S(2)}) async-start(bf16[32,32,512]{2,1,0:T(8,128)(2,1)} %bitcast.139), calls=%async_computation.5 | async-start | bytes 2097152 | tf_op jit(solution)/shard_map/all_to_all | solution.py:497
  272.6 7.0 %copy-start.7 = (f32[256,1024]{1,0:T(8,128)S(1)}, f32[256,1024]{1,0:T(8,128)}, u32[]{:S(2)}) copy-start(f32[256,1024]{1,0:T(8,128)} %copy-done.6) | copy-start | bytes 3145732
  276.4 15.6 %collective-permute-start.4 = (bf16[4,128,1024]{2,1,0:T(8,128)(2,1)}, bf16[4,128,1024]{2,1,0:T(8,128)(2,1)S(1)}, u32[]{:S(2)}, u32[]{:S(2)}) collective-permute-start(bf16[4,128,1024]{2,1,0:T(8,128)(2,1)} %bitcast.36), channel_id=1, source_target_pairs={{0,32},{32,0},{1,33},{33,1},{2,34},{34,2},{3,35},{35,3},{4,36},{36... | collective-permute-start | bytes 3145736 | tf_op jit(solution)/shard_map/ppermute | solution.py:501
  279.6 13.4 %copy-start.15 = (bf16[512,1024]{1,0:T(8,128)(2,1)S(1)}, bf16[512,1024]{1,0:T(8,128)(2,1)}, u32[]{:S(2)}) copy-start(bf16[512,1024]{1,0:T(8,128)(2,1)} %get-tuple-element.115) | copy-start | bytes 3145732
  279.7 17.9 %collective-permute-start.5 = (bf16[4,128,1024]{2,1,0:T(8,128)(2,1)}, bf16[4,128,1024]{2,1,0:T(8,128)(2,1)}, u32[]{:S(2)}, u32[]{:S(2)}) collective-permute-start(bf16[4,128,1024]{2,1,0:T(8,128)(2,1)} %bitcast.39), channel_id=1, source_target_pairs={{0,32},{32,0},{1,33},{33,1},{2,34},{34,2},{3,35},{35,3},{4,36},{36... | collective-permute-start | bytes 3145736 | tf_op jit(solution)/shard_map/ppermute | solution.py:501
  279.8 2.7 collective-permute-start.6
  280.4 36.3 %copy-start.18 = (f32[2,32,512]{2,1,0:T(8,128)}, f32[2,32,512]{2,1,0:T(8,128)S(1)}, u32[]{:S(2)}) copy-start(f32[2,32,512]{2,1,0:T(8,128)S(1)} %get-tuple-element.134) | copy-start | bytes 393220
  288.6 11.5 %all-to-all-start.6 = ((bf16[8,16,1024]{2,1,0:T(8,128)(2,1)}), bf16[8,16,1024]{2,1,0:T(8,128)(2,1)S(1)}, u32[]{:S(2)}, u32[]{:S(2)}) async-start(bf16[8,16,1024]{2,1,0:T(8,128)(2,1)} %pad_maximum_fusion.5), calls=%async_computation.6 | async-start | bytes 524288 | tf_op jit(solution)/shard_map/all_to_all | solution.py:497
  295.5 7.0 %collective-permute-start.9 = (bf16[128,1024]{1,0:T(8,128)(2,1)}, bf16[128,1024]{1,0:T(8,128)(2,1)S(1)}, u32[]{:S(2)}, u32[]{:S(2)}) collective-permute-start(bf16[128,1024]{1,0:T(8,128)(2,1)} %get-tuple-element.122), channel_id=1, source_target_pairs={{0,16},{8,24},{16,0},{24,8},{1,17},{9,25},{17,1},{25,9},{2,18},{10... | collective-permute-start | bytes 786440 | tf_op jit(solution)/shard_map/ppermute | solution.py:509
  296.0 11.5 %collective-permute-start.8 = (bf16[128,1024]{1,0:T(8,128)(2,1)S(1)}, bf16[128,1024]{1,0:T(8,128)(2,1)S(1)}, u32[]{:S(2)}, u32[]{:S(2)}) collective-permute-start(bf16[128,1024]{1,0:T(8,128)(2,1)S(1)} %get-tuple-element.123), channel_id=1, source_target_pairs={{0,24},{8,0},{16,8},{24,16},{1,25},{9,1},{17,9},{25,17},{2,26},{10... | collective-permute-start | bytes 786440 | tf_op jit(solution)/shard_map/ppermute | solution.py:509
  297.5 12.0 %collective-permute-start.7 = (bf16[128,1024]{1,0:T(8,128)(2,1)S(1)}, bf16[128,1024]{1,0:T(8,128)(2,1)S(1)}, u32[]{:S(2)}, u32[]{:S(2)}) collective-permute-start(bf16[128,1024]{1,0:T(8,128)(2,1)S(1)} %get-tuple-element.124), channel_id=1, source_target_pairs={{0,8},{8,16},{16,24},{24,0},{1,9},{9,17},{17,25},{25,1},{2,10},{10... | collective-permute-start | bytes 786440 | tf_op jit(solution)/shard_map/ppermute | solution.py:509
  300.1 10.2 %copy-start.22 = (bf16[8,16,1024]{2,1,0:T(8,128)(2,1)}, bf16[8,16,1024]{2,1,0:T(8,128)(2,1)S(1)}, u32[]{:S(2)}) copy-start(bf16[8,16,1024]{2,1,0:T(8,128)(2,1)S(1)} %all-to-all-done.6) | copy-start | bytes 786436
  302.5 7.8 %copy-start.25 = (bf16[128,1024]{1,0:T(8,128)(2,1)}, bf16[128,1024]{1,0:T(8,128)(2,1)S(1)}, u32[]{:S(2)}) copy-start(bf16[128,1024]{1,0:T(8,128)(2,1)S(1)} %collective-permute-done.9) | copy-start | bytes 786436
  310.3 18.4 %all-to-all-start.7 = ((bf16[4,128,1024]{2,1,0:T(8,128)(2,1)}), bf16[4,128,1024]{2,1,0:T(8,128)(2,1)S(1)}, u32[]{:S(2)}, u32[]{:S(2)}) async-start(bf16[4,128,1024]{2,1,0:T(8,128)(2,1)} %fusion.1), calls=%async_computation.8 | async-start | bytes 2097152 | tf_op jit(solution)/shard_map/all_to_all | solution.py:497
  317.5 11.2 %collective-permute-start.10 = (bf16[208,1024]{1,0:T(8,128)(2,1)}, bf16[208,1024]{1,0:T(8,128)(2,1)}, u32[]{:S(2)}, u32[]{:S(2)}) collective-permute-start(bf16[208,1024]{1,0:T(8,128)(2,1)} %fusion.26), channel_id=1, source_target_pairs={{0,64},{64,0},{1,65},{65,1},{2,66},{66,2},{3,67},{67,3},{4,68},{68... | collective-permute-start | bytes 1277960 | tf_op jit(solution)/shard_map/ppermute | solution.py:770
  320.8 12.9 %copy-start.16 = (bf16[128,1024]{1,0:T(8,128)(2,1)S(1)}, bf16[128,1024]{1,0:T(8,128)(2,1)}, u32[]{:S(2)}) copy-start(bf16[128,1024]{1,0:T(8,128)(2,1)} %param.31) | copy-start | bytes 786436
  330.6 5.5 %collective-permute-start.11 = (f32[208,1024]{1,0:T(8,128)S(1)}, f32[208,1024]{1,0:T(8,128)S(1)}, u32[]{:S(2)}, u32[]{:S(2)}) collective-permute-start(f32[208,1024]{1,0:T(8,128)S(1)} %convert_add_fusion.2.mine), channel_id=1, source_target_pairs={{0,32},{32,0},{1,33},{33,1},{2,34},{34,2},{3,35},{35,3},{4,36},{36... | collective-permute-start | bytes 2555912 | tf_op jit(solution)/shard_map/ppermute | solution.py:501
  (32 other events, 116.4 us)
Sparse Core Ops, SparseCore 0:
  19.6 62.0 all-gather.2
  212.6 52.7 reduce-scatter.1
